TPU v7x, 128 devices: a whole 4x4x4 slice. The times are simulated.
128 devices in a mesh: seq: 16 (over z, x), head: 8 (over y, core).
Axes of the slice: x: 4, y: 4, z: 4, core: 2. Of those that a mesh axis runs over, the one named last changes fastest.
Arguments:
- tokens: bfloat16 [8192, 3072], P(('seq', 'head')), may hold values from -6 to 6
- block_target: int32 [512], replicated, may hold values from 0 to 15, as said below
- clip_within: int32 [512], replicated, may hold values from 0 to 3, as said below
- modulation: float32 [64, 3, 3072], P('seq'), may hold values from -6 to 6
- inner_attention: bfloat16 [3072, 3, 2048], P(None, None, 'head'), may hold values from -0.109375 to 0.109375
- inner_hidden: bfloat16 [3072, 6144], P(None, 'head'), may hold values from -0.109375 to 0.109375
- outer_attention: bfloat16 [2048, 3072], P('head'), may hold values from -0.125 to 0.125
- outer_hidden: bfloat16 [6144, 3072], P('head'), may hold values from -0.078125 to 0.078125
Outputs:
- mixed_tokens: bfloat16 [8192, 3072], P(('seq', 'head'))
Inputs may be any that keep to these rules, and one draw needn't show every extreme that they name: `block_target`: the 4 blocks of one device go to different seq indices. Counting only the devices of one head index, each seq index receives 2 to 6 blocks, and some seq index receives exactly 6 of them. `clip_within`: blocks with the same target and the same number form one clip; at each seq index the numbers never fall along the block order, and its first block has number 0 and its last 3.
All inputs are finite; a program needn't handle non-finite values.
Results may differ from a plain program's by a relative error of at most 0.017.
Values may be sent and summed in bfloat16 or wider, within the bound.
A program may use at most 128 MiB of HBM per device.

v0:
```python
import jax
import jax.numpy as jnp
from jax import lax
from jax.sharding import PartitionSpec as P

HD = 128
BLOCK = 16
BLK_DEV = 4
CPG = 4
RCAP = 6


EPSILON = 1e-06


def layer_norm(values):
    centred = values - jnp.mean(values, axis=-1, keepdims=True)
    return centred * lax.rsqrt(jnp.mean(centred * centred, axis=-1, keepdims=True) + EPSILON)


def rms_norm(values):
    return values * lax.rsqrt(jnp.mean(values * values, axis=-1, keepdims=True) + EPSILON)


def modulate(rows, row_clips, modulation, first_clip):
    local = row_clips - first_clip
    match = local[:, None] == jnp.arange(modulation.shape[0], dtype=jnp.int32)[None, :]
    picked = jnp.sum(jnp.where(match[:, :, None, None], modulation[None], 0.0), axis=1)
    shaped = (
        layer_norm(rows.astype(jnp.float32)) * (1.0 + picked[:, 1][:, None, :])
        + picked[:, 0][:, None, :]
    )
    return (shaped.astype(jnp.bfloat16), picked[:, 2])


def block_count():
    return 1


def attend(queries, keys_all, values_all, token_clip):
    rows, heads_dev, depth = queries.shape
    pieces = block_count()
    length = rows // pieces
    scale = depth ** (-0.5)

    def one_block(item):
        query, clip_query = item
        scores = (
            jnp.einsum("qhd,khd->hqk", query, keys_all, preferred_element_type=jnp.float32) * scale
        )
        mask = clip_query[:, None] == token_clip[None, :]
        powers = jnp.where(mask[None], jnp.exp(scores), 0.0)
        weights = (powers / jnp.sum(powers, axis=-1, keepdims=True)).astype(jnp.bfloat16)
        mixed = jnp.einsum("hqk,khd->qhd", weights, values_all, preferred_element_type=jnp.float32)
        return mixed.astype(jnp.bfloat16).reshape(length, heads_dev * depth)

    outcome = lax.map(
        one_block,
        (queries.reshape(pieces, length, heads_dev, depth), token_clip.reshape(pieces, length)),
    )
    return outcome.reshape(rows, heads_dev * depth)


def body(
    tokens,
    block_target,
    clip_within,
    modulation,
    inner_attention,
    inner_hidden,
    outer_attention,
    outer_hidden,
):
    seq_count = lax.axis_size("seq")
    head_count = lax.axis_size("head")
    seq_index = lax.axis_index("seq")
    head_index = lax.axis_index("head")
    width = tokens.shape[1]
    blocks = tokens.reshape(BLK_DEV, BLOCK, width)
    targets = block_target.reshape(seq_count, head_count, BLK_DEV)
    clip_ids = targets * CPG + clip_within.reshape(seq_count, head_count, BLK_DEV)
    groups = jnp.arange(seq_count, dtype=jnp.int32)
    chosen = (targets[..., None] == groups).astype(jnp.int32)
    sent = jnp.sum(chosen, axis=2)
    ranks = jnp.cumsum(sent, axis=0) - sent
    mine_sent = jnp.take(sent, seq_index, axis=2)
    mine_rank = jnp.take(ranks, seq_index, axis=2)
    to_me = targets == seq_index
    slot_number = jnp.arange(RCAP, dtype=jnp.int32)
    hit = to_me[..., None] & (mine_rank[:, :, None, None] == slot_number)
    slot_clip = jnp.sum(jnp.where(hit, clip_ids[..., None] + 1, 0), axis=(0, 2)) - 1
    sources = jnp.arange(seq_count, dtype=jnp.int32)[:, None, None, None]
    slot_source = jnp.sum(jnp.where(hit, sources, 0), axis=(0, 2))
    slot_live = jnp.sum(hit.astype(jnp.int32), axis=(0, 2))
    first_clip = seq_index * CPG
    own_targets = targets[seq_index, head_index]
    send_match = own_targets[None, :] == groups[:, None]
    send_block = jnp.sum(
        jnp.where(send_match, jnp.arange(BLK_DEV, dtype=jnp.int32)[None, :], 0), axis=1
    )
    send_live = jnp.sum(send_match.astype(jnp.int32), axis=1)
    outgoing = jnp.take(blocks, send_block, axis=0) * send_live[:, None, None].astype(jnp.bfloat16)
    attention_flat = inner_attention.reshape(width, -1)
    fanned = jnp.broadcast_to(outgoing[:, None], (seq_count, head_count, BLOCK, width))
    fanned = fanned.reshape(seq_count * head_count, BLOCK, width)
    received = lax.all_to_all(fanned, ("seq", "head"), split_axis=0, concat_axis=0, tiled=True)
    flat_index = slot_source * head_count + jnp.arange(head_count, dtype=jnp.int32)[:, None]
    group_rows = jnp.take(received, flat_index.reshape(-1), axis=0)
    group_rows = group_rows * slot_live.reshape(-1)[:, None, None].astype(jnp.bfloat16)
    group_mod, group_gate = modulate(group_rows, slot_clip.reshape(-1), modulation, first_clip)
    piece = group_mod.reshape(-1, width)
    first = jnp.dot(piece, attention_flat, preferred_element_type=jnp.float32)
    second = jnp.dot(piece, inner_hidden, preferred_element_type=jnp.float32)
    projected = jnp.concatenate([first, second], axis=1)
    own_rows = jnp.take(group_rows.reshape(head_count, RCAP, BLOCK, width), head_index, axis=0)
    own_gate = jnp.take(group_gate.reshape(head_count, RCAP, width), head_index, axis=0)
    qkv_width = attention_flat.shape[1]
    heads_dev = qkv_width // (3 * HD)
    row_total = projected.shape[0]
    triple = projected[:, :qkv_width].reshape(row_total, 3, heads_dev, HD)
    queries = rms_norm(triple[:, 0]).astype(jnp.bfloat16)
    keys_all = rms_norm(triple[:, 1]).astype(jnp.bfloat16)
    values_all = triple[:, 2].astype(jnp.bfloat16)
    hidden = jax.nn.gelu(projected[:, qkv_width:], approximate=True).astype(jnp.bfloat16)
    token_clip = jnp.repeat(slot_clip.reshape(-1), BLOCK)
    attended = attend(queries, keys_all, values_all, token_clip)
    first = jnp.dot(attended, outer_attention, preferred_element_type=jnp.float32)
    branch = lax.psum_scatter(
        (first + jnp.dot(hidden, outer_hidden, preferred_element_type=jnp.float32)).astype(
            jnp.bfloat16
        ),
        "head",
        scatter_dimension=0,
        tiled=True,
    ).astype(jnp.float32)
    finished = own_rows.astype(jnp.float32) + own_gate[:, None, :] * branch.reshape(
        RCAP, BLOCK, width
    )
    finished = finished.astype(jnp.bfloat16)
    back_rank = jnp.minimum(jnp.take(mine_rank, head_index, axis=1), RCAP - 1)
    back_live = jnp.take(mine_sent, head_index, axis=1)
    returning = jnp.take(finished, back_rank, axis=0) * back_live[:, None, None].astype(
        jnp.bfloat16
    )
    arrived = lax.all_to_all(returning, "seq", split_axis=0, concat_axis=0, tiled=True)
    return jnp.take(arrived, own_targets, axis=0).reshape(BLK_DEV * BLOCK, width)


def solution(mesh):
    placed = (
        P(("seq", "head"), None),
        P(),
        P(),
        P("seq", None, None),
        P(None, None, "head"),
        P(None, "head"),
        P("head", None),
        P("head", None),
    )
    return jax.shard_map(
        body, mesh=mesh, in_specs=placed, out_specs=P(("seq", "head"), None), check_vma=False
    )
```

profile of v0, /device:TPU:0, one launch (start us, length us, event | category | flops | bytes accessed | tf_op | source)
XLA Modules:
  0.0 327.9 jit_solution(6627306517445116432)
XLA Ops:
  6.5 0.9 reshape.416
  7.5 0.1 convert_reduce_fusion.2
  7.6 2.8 gather_fusion
  10.4 1.6 select_multiply_fusion.2
  12.0 6.1 %broadcast_in_dim.215 = bf16[16,8,16,3072]{3,2,1,0:T(8,128)(2,1)} broadcast(bf16[16,16,3072]{2,1,0:T(8,128)(2,1)S(1)} %select_multiply_fusion.2), dimensions={0,2,3} | broadcast | bytes 14155776 | tf_op jit(solution)/shard_map/broadcast_in_dim | solution.py:104
  18.1 11.6 %all-to-all-start = ((bf16[128,16,3072]{2,1,0:T(8,128)(2,1)}), bf16[128,16,3072]{2,1,0:T(8,128)(2,1)}, u32[]{:S(2)}, u32[]{:S(2)}) async-start(bf16[128,16,3072]{2,1,0:T(8,128)(2,1)} %bitcast.101), calls=%async_computation | async-start | bytes 25165824 | tf_op jit(solution)/shard_map/all_to_all | solution.py:106
  29.8 0.2 copy.24
  29.9 0.1 convert_reduce_fusion.1
  30.1 0.7 fusion.56
  30.8 0.1 dynamic-slice_select_fusion.1
  30.9 0.1 copy.25
  31.0 0.1 copy.26
  31.2 0.1 reshape.419
  31.3 0.1 copy.30
  31.4 0.4 fusion.38
  31.9 0.1 copy.28
  32.1 0.1 copy.29
  32.2 0.1 convert_element_type.101
  32.5 0.1 copy.32
  32.6 6.7 %copy.35 = bf16[3072,3,256]{0,2,1:T(8,128)(2,1)} copy(bf16[3072,3,256]{2,0,1:T(8,128)(2,1)} %param.16) | data formatting | bytes 9437184 | tf_op args[4]
  39.5 0.1 broadcast_in_dim.230
  39.6 0.1 mul.207
  39.8 1.3 broadcast_compare_fusion
  41.0 0.7 select_reduce_fusion
  41.7 0.1 fusion.53
  41.9 139.7 %all-to-all-done = bf16[128,16,3072]{2,1,0:T(8,128)(2,1)} async-done(((bf16[128,16,3072]{2,1,0:T(8,128)(2,1)}), bf16[128,16,3072]{2,1,0:T(8,128)(2,1)}, u32[]{:S(2)}, u32[]{:S(2)}) %all-to-all-start) | async-done | bytes 12582944 | tf_op jit(solution)/shard_map/all_to_all | solution.py:106
  181.6 7.7 %gather_fusion.1 = bf16[48,16,3072]{2,1,0:T(8,128)(2,1)} fusion(bf16[128,16,3072]{2,1,0:T(8,128)(2,1)} %all-to-all-done, s32[1024]{0:T(1024)S(1)} %pad_clamp_fusion.2), kind=kCustom, calls=%fused_computation.1 | custom fusion | bytes 9437376 | tf_op jit(solution)/shard_map/jit(_take)/gather | solution.py:108
  189.3 5.9 %convert_reduce_fusion = (f32[48,16]{1,0:T(8,128)S(1)}, bf16[48,16,3072]{2,1,0:T(8,128)(2,1)}) fusion(bf16[48]{0:T(256)(128)(2,1)S(1)} %convert_element_type.101, bf16[48,16,3072]{2,1,0:T(8,128)(2,1)} %gather_fusion.1, pred[48]{0:T(512)(128)(4,1)S(1)} %compare_and_fusion.1), kind=kLoop, calls=%fused_computation.5 | loop fusion | flops 9436416 | bytes 9440400 | tf_op jit(solution)/shard_map/reduce_sum | solution.py:17
  195.3 3.7 %fusion.2 = f32[48,16]{1,0:T(8,128)S(1)} fusion(bf16[48,16,3072]{2,1,0:T(8,128)(2,1)} %get-tuple-element.84, f32[48,16]{1,0:T(8,128)S(1)} %broadcast_multiply_fusion), kind=kLoop, calls=%fused_computation.8 | loop fusion | flops 9436416 | bytes 4724736 | tf_op jit(solution)/shard_map/reduce_sum | solution.py:18
  199.1 4.5 %fusion.5 = bf16[48,16,3072]{2,1,0:T(8,128)(2,1)S(1)} fusion(bf16[48,16,3072]{2,1,0:T(8,128)(2,1)} %get-tuple-element.84, f32[48,3072]{1,0:T(8,128)S(1)} %get-tuple-element.86, f32[48,3072]{1,0:T(8,128)S(1)} %get-tuple-element.87, f32[48,16]{1,0:T(8,128)S(1)} %add_rsqrt_fusion, f32[48,16]{1,0:T(8,128)S(1)} %broadcast_multiply_fusion), kind=kLoop, calls=%fused_computation.11 | loop fusion | flops 14155776 | bytes 10622976 | tf_op jit(solution)/shard_map/convert_element_type | solution.py:33
  203.6 5.9 %fusion.57 = f32[768,3,2,128]{0,3,2,1:T(8,128)S(1)} fusion(bf16[768,3072,1,1]{1,0,3,2:T(8,128)(2,1)S(1)} %bitcast.107, bf16[3,2,128,3072]{3,2,1,0:T(8,128)(2,1)} %bitcast.106), kind=kOutput, calls=%fused_computation.130 | convolution fusion | flops 3623878656 | bytes 11796480 | tf_op jit(solution)/shard_map/dot_general | solution.py:112
  209.5 0.1 multiply_reduce_fusion.1
  209.7 1.4 fusion.8
  211.1 2.3 fusion.18
  213.4 5.7 %fusion.6 = bf16[768,3072]{1,0:T(8,128)(2,1)} fusion(bf16[48,16,3072]{2,1,0:T(8,128)(2,1)S(1)} %bitcast.104, f32[768]{0:T(1024)S(1)} %rsqrt.31, f32[768]{0:T(1024)S(1)} %div.32, f32[48,3072]{1,0:T(8,128)S(1)} %get-tuple-element.86, f32[48,3072]{1,0:T(8,128)S(1)} %get-tuple-element.87, pred[768]{0:T(1024)(128)(4,1)S(1)} %broadcast_in_dim.230, ...), kind=kLoop, calls=%fused_computation.13 | loop fusion | flops 18874368 | bytes 10625280 | tf_op jit(solution)/shard_map/convert_element_type | solution.py:33
  219.1 16.5 %fusion.19 = f32[768,3072]{1,0:T(8,128)} fusion(bf16[768,3072]{1,0:T(8,128)(2,1)} %param.19, bf16[768,3072]{1,0:T(8,128)(2,1)} %fusion.6, bf16[3072,768]{1,0:T(8,128)(2,1)} %param.17), kind=kOutput, calls=%fused_computation.36 | convolution fusion | flops 7253065728 | bytes 23592960 | tf_op jit(solution)/shard_map/dot_general | solution.py:129
  235.6 7.3 %add_convert_fusion = bf16[768,3072]{1,0:T(8,128)(2,1)} fusion(f32[768,3072]{1,0:T(8,128)} %fusion.19, bf16[768,256]{0,1:T(8,128)(2,1)S(1)} %bitcast.109, bf16[256,3072]{1,0:T(8,128)(2,1)S(1)} %copy-done), kind=kOutput, calls=%fused_computation.15 | convolution fusion | flops 1212678144 | bytes 16121856 | tf_op jit(solution)/shard_map/dot_general | solution.py:127
  243.0 0.1 copy.27
  243.1 0.1 copy.39
  243.3 42.1 %reduce-scatter.2.cloned.1.call-done = bf16[96,3072]{1,0:T(8,128)(2,1)} async-done(((bf16[768,3072]{1,0:T(8,128)(2,1)}), bf16[96,3072]{1,0:T(8,128)(2,1)}) %reduce-scatter.2.cloned.1.call-update) | async-done | bytes 589840 | tf_op jit(solution)/shard_map/reduce_scatter | solution.py:128
  285.4 1.6 fusion.22
  287.0 1.8 gather_fusion.2
  288.8 2.8 select_multiply_fusion.1
  291.6 6.9 %all-to-all-start.1 = ((bf16[16,16,3072]{2,1,0:T(8,128)(2,1)}), bf16[16,16,3072]{2,1,0:T(8,128)(2,1)S(1)}, u32[]{:S(2)}, u32[]{:S(2)}) async-start(bf16[16,16,3072]{2,1,0:T(8,128)(2,1)} %select_multiply_fusion.1), calls=%async_computation.2 | async-start | bytes 3145728 | tf_op jit(solution)/shard_map/all_to_all | solution.py:145
  298.5 0.1 broadcast_in_dim.203
  298.6 21.0 %all-to-all-done.1 = bf16[16,16,3072]{2,1,0:T(8,128)(2,1)S(1)} async-done(((bf16[16,16,3072]{2,1,0:T(8,128)(2,1)}), bf16[16,16,3072]{2,1,0:T(8,128)(2,1)S(1)}, u32[]{:S(2)}, u32[]{:S(2)}) %all-to-all-start.1) | async-done | bytes 1572896 | tf_op jit(solution)/shard_map/all_to_all | solution.py:145
  319.6 0.6 gather_fusion.3
  320.2 0.9 bitcast_select_fusion.1
  (57 shorter events, 1.3 us)
Async XLA Ops:
  6.5 229.1 %copy-start = (bf16[256,3072]{1,0:T(8,128)(2,1)S(1)}, bf16[256,3072]{1,0:T(8,128)(2,1)}, u32[]{:S(2)}) copy-start(bf16[256,3072]{1,0:T(8,128)(2,1)} %param.18) | copy-start | bytes 4718596
  18.1 13.1 %copy-start.4 = (s32[512]{0:T(512)S(1)}, s32[512]{0:T(512)}, u32[]{:S(2)}) copy-start(s32[512]{0:T(512)} %param.14) | copy-start | bytes 6148
  18.1 14.4 %copy-start.3 = (f32[4,3,3072]{2,0,1:T(4,128)S(1)}, f32[4,3,3072]{2,0,1:T(4,128)}, u32[]{:S(2)}) copy-start(f32[4,3,3072]{2,0,1:T(4,128)} %param.15) | copy-start | bytes 442372
  18.1 163.5 %all-to-all-start = ((bf16[128,16,3072]{2,1,0:T(8,128)(2,1)}), bf16[128,16,3072]{2,1,0:T(8,128)(2,1)}, u32[]{:S(2)}, u32[]{:S(2)}) async-start(bf16[128,16,3072]{2,1,0:T(8,128)(2,1)} %bitcast.101), calls=%async_computation | async-start | bytes 25165824 | tf_op jit(solution)/shard_map/all_to_all | solution.py:106
  29.7 255.7 %reduce-scatter.2.cloned.1.call-start = ((), (), s32[]{:S(2)}) async-start(), calls=%async_computation.3 | async-start | bytes 5308416 | tf_op jit(solution)/shard_map/reduce_scatter | solution.py:128
  203.6 6.1 %copy-start.1 = (pred[768,768]{0,1:T(8,128)(4,1)S(1)}, pred[768,768]{0,1:T(8,128)(4,1)}, u32[]{:S(2)}) copy-start(pred[768,768]{0,1:T(8,128)(4,1)} %broadcast_compare_fusion) | copy-start | bytes 1769476
  209.7 3.7 %slice-start = ((s8[4718592]{0:T(1024)(128)(4,1)}), s8[4194304]{0:T(1024)(128)(4,1)S(1)}, s32[]{:S(2)}) async-start(s8[4718592]{0:T(1024)(128)(4,1)} %bitcast.103), calls=%async_computation.4 | async-start | bytes 8388608
  211.1 2.3 slice-start.1
  219.1 16.6 %copy-start.2 = (bf16[2,128,768]{2,1,0:T(8,128)(2,1)S(1)}, bf16[2,128,768]{2,1,0:T(8,128)(2,1)}, u32[]{:S(2)}) copy-start(bf16[2,128,768]{2,1,0:T(8,128)(2,1)} %fusion.18) | copy-start | bytes 1179652
  291.6 28.1 %all-to-all-start.1 = ((bf16[16,16,3072]{2,1,0:T(8,128)(2,1)}), bf16[16,16,3072]{2,1,0:T(8,128)(2,1)S(1)}, u32[]{:S(2)}, u32[]{:S(2)}) async-start(bf16[16,16,3072]{2,1,0:T(8,128)(2,1)} %select_multiply_fusion.1), calls=%async_computation.2 | async-start | bytes 3145728 | tf_op jit(solution)/shard_map/all_to_all | solution.py:145
Sparse Core Ops, SparseCore 0:
  243.0 42.3 reduce-scatter.1
where the time goes:
time: 330 us; the launch traced here: 328 us
  waiting for transfers between devices  203 us (62%)
  matrix products  33.4 us (10%)
  other arithmetic  30.4 us (9%)
  local copies, waits for them, and re-layouts  29 us (9%)
  starting transfers between devices  18.5 us (6%)
  between operations  13.8 us (4%)
    all_to_all x1, waiting for transfers between devices, body(): lax.all_to_all(fanned, ('seq', 'head'), split_axis=0, concat_axis=0, tile...  140 us
    reduce_scatter x1, waiting for transfers between devices, body(): lax.psum_scatter((first + jnp.dot(hidden, outer_hidden, preferred_element...  42.1 us
    all_to_all x1, waiting for transfers between devices, body(): lax.all_to_all(returning, 'seq', split_axis=0, concat_axis=0, tiled=True)  21 us
    dot_general x1, matrix products, body(): jnp.dot(hidden, outer_hidden, preferred_element_type=jnp.float32)  16.5 us
    all_to_all x1, starting transfers between devices, body(): lax.all_to_all(fanned, ('seq', 'head'), split_axis=0, concat_axis=0, tile...  11.6 us
    convert_element_type x2, other arithmetic, modulate(): return (shaped.astype(jnp.bfloat16), picked[:, 2])  10.1 us
    gather x1, local copies, waits for them, and re-layouts, body(): group_rows = jnp.take(received, flat_index.reshape(-1), axis=0)  7.68 us
    dot_general x1, matrix products, body(): jnp.dot(attended, outer_attention, preferred_element_type=jnp.float32)  7.26 us
  transfers between devices with their start and end apart: 3, of which 3 were waited for; matrix products, arithmetic and copies ran while one was open for 4% of the time, Pallas kernels for 0%

commit v1 on v0

v1 whole, which is shorter than its diff:
```python
import math

import jax
import jax.numpy as jnp
from jax import lax
from jax.experimental import pallas as pl
from jax.experimental.pallas import tpu as pltpu
from jax.sharding import PartitionSpec as P

MESH = pl.DeviceIdType.MESH
F32 = jnp.float32
BF16 = jnp.bfloat16

HD = 128
BLOCK = 16
BLK_DEV = 4
CPG = 4
RCAP = 6
EPSILON = 1e-06

Z = 4
X = 4
NSEQ = Z * X
Y = 4
NHEAD = 8
D = 3072
ROWS = RCAP * BLOCK
ALL = NHEAD * ROWS
HALF = ROWS // 2
NC = 4
CC = D // NC
TILE = 256
QT = 256
NT = CC // TILE
ATT = 256
HID = 768
BIG = 1536.0
EXP_A = HD ** (-0.5) * math.log2(math.e)
EXP_B = BIG * EXP_A

OFFSETS = sorted(
    [(a, b) for a in range(Z) for b in range(X) if (a, b) != (0, 0)],
    key=lambda o: -(min(o[0], Z - o[0]) + min(o[1], X - o[1])),
)


def kernel(
    bt, cw, tok, md, wq, wh, woa, woh, out,
    nrm, inbox, st_a, rv_a, gath, win, wo, acc, qa, ka, va, ah,
    term, rv_s, rv_f, rv_n, fin, st_e, rv_e, ranks, srcs, clips,
    w_sem, ss_a, rs_a, ss_b, rs_b, ss_g, rs_g,
    ss_s, rs_s, ss_f, rs_f, ss_n, rs_n, ss_e, rs_e,
):
    me = lax.axis_index("seq")
    head = lax.axis_index("head")
    z, x = me // X, me % X
    y, core = head // 2, head % 2
    sibling = head + 1 - 2 * core
    group = core * Y + y

    def seq_at(dz, dx):
        return ((z + dz) % Z) * X + (x + dx) % X

    def head_at(dy):
        return ((y + dy) % Y) * 2 + core

    def remote(src, dst, ss, rs, dev):
        return pltpu.make_async_remote_copy(
            src_ref=src, dst_ref=dst, send_sem=ss, recv_sem=rs, device_id=dev, device_id_type=MESH
        )

    loads = [
        pltpu.make_async_copy(wq, win.at[pl.ds(0, 3)], w_sem.at[0]),
        pltpu.make_async_copy(woa, wo.at[pl.ds(0, ATT)], w_sem.at[1]),
        pltpu.make_async_copy(woh, wo.at[pl.ds(ATT, HID)], w_sem.at[2]),
    ] + [
        pltpu.make_async_copy(wh.at[:, pl.ds(n * TILE, TILE)], win.at[3 + n], w_sem.at[3 + n])
        for n in range(3)
    ]
    for load in loads:
        load.start()

    barrier = pltpu.get_barrier_semaphore()
    for dz, dx in OFFSETS:
        pl.semaphore_signal(barrier, inc=1, device_id=(seq_at(dz, dx), head), device_id_type=MESH)
    for dy in range(1, Y):
        pl.semaphore_signal(barrier, inc=1, device_id=(me, head_at(dy)), device_id_type=MESH)
    pl.semaphore_signal(barrier, inc=1, device_id=(me, sibling), device_id_type=MESH)

    for j in range(BLK_DEV):
        rows = tok[j * BLOCK : (j + 1) * BLOCK, :].astype(F32)
        centred = rows - jnp.mean(rows, axis=-1, keepdims=True)
        scale = lax.rsqrt(jnp.mean(centred * centred, axis=-1, keepdims=True) + EPSILON)
        nrm[j] = (centred * scale).astype(BF16)
    base = (me * NHEAD + head) * BLK_DEV
    targets = [bt[base + j] for j in range(BLK_DEV)]

    def stage(t, carry):
        pick = jnp.int32(0)
        for j in range(1, BLK_DEV):
            pick = jnp.where(targets[j] == t, j, pick)
        block = nrm[pick]
        for c in range(NC):
            st_a[c, t] = block[:, c * CC : (c + 1) * CC]
        return carry

    lax.fori_loop(0, NSEQ, stage, 0)
    pl.semaphore_wait(barrier, NSEQ - 1 + Y)

    def send_a(c, k):
        to = seq_at(*OFFSETS[k])
        return remote(st_a.at[c, to], rv_a.at[c, me], ss_a.at[c, k], rs_a.at[c, k], (to, head))

    def got_a(c, k):
        dz, dx = OFFSETS[k]
        frm = seq_at(Z - dz, X - dx)
        return remote(st_a.at[c, frm], rv_a.at[c, frm], ss_a.at[c, k], rs_a.at[c, k], (frm, head))

    def start_a(c, carry):
        for k in range(NSEQ - 1):
            send_a(c, k).start()
        rv_a[c, me] = st_a[c, me]
        return carry

    lax.fori_loop(0, NC, start_a, 0)

    def entry(s, h):
        live, clip = jnp.int32(0), jnp.int32(0)
        for j in range(BLK_DEV):
            at = (s * NHEAD + h) * BLK_DEV + j
            hit = bt[at] == me
            live = jnp.where(hit, 1, live)
            clip = jnp.where(hit, cw[at], clip)
        return live, clip

    def own_slot(s, carry):
        count, picked, named = carry
        live, clip = entry(s, head)
        ranks[s] = jnp.minimum(count, RCAP - 1)
        at = jnp.where(live == 1, count, -1)
        picked = tuple(jnp.where(at == r, s, picked[r]) for r in range(RCAP))
        named = tuple(jnp.where(at == r, clip, named[r]) for r in range(RCAP))
        return count + live, picked, named

    zeros = (jnp.int32(0),) * RCAP
    _, picked, named = lax.fori_loop(0, NSEQ, own_slot, (jnp.int32(0), zeros, zeros))
    for r in range(RCAP):
        srcs[r] = picked[r]
        clips[r] = named[r]

    lanes = lax.broadcasted_iota(jnp.int32, (BLOCK, HD), 1)

    def group_slots(g, carry):
        h = (g % Y) * 2 + g // Y

        def slot(s, carry):
            count, named = carry
            live, clip = entry(s, h)
            at = jnp.where(live == 1, count, -1)
            return count + live, tuple(jnp.where(at == r, clip, named[r]) for r in range(RCAP))

        dead = (jnp.int32(CPG),) * RCAP
        _, named = lax.fori_loop(0, NSEQ, slot, (jnp.int32(0), dead))
        for r in range(RCAP):
            one = jnp.where(lanes == named[r], 1.0, 0.0)
            at = pl.ds(pl.multiple_of(g * ROWS + r * BLOCK, BLOCK), BLOCK)
            for i in range(2):
                qa[i, at, HD:] = (one * BIG).astype(BF16)
                ka[i, at, HD:] = one.astype(BF16)
                va[i, at, HD:] = jnp.ones((BLOCK, HD), BF16)
        return carry

    lax.fori_loop(0, NHEAD, group_slots, 0)

    def clear(n, carry):
        acc[n] = jnp.zeros((ALL, TILE), F32)
        return carry

    lax.fori_loop(0, 6, clear, 0)

    def own_rows(c):
        return gath.at[c, group]

    def rows_of(c, dy):
        return gath.at[c, core * Y + (y + dy) % Y]

    def rows_of_sibling(c, dy):
        return gath.at[c, (1 - core) * Y + (y + dy) % Y]

    def send_b(c, k):
        return remote(own_rows(c), own_rows(c), ss_b.at[c, k], rs_b.at[c, k], (me, head_at(k)))

    def got_b(c, k):
        ref = rows_of(c, Y - k)
        return remote(ref, ref, ss_b.at[c, k], rs_b.at[c, k], (me, head_at(Y - k)))

    def send_g(c, k):
        ref = rows_of(c, Y - k)
        return remote(ref, ref, ss_g.at[c, k], rs_g.at[c, k], (me, sibling))

    def got_g(c, k):
        ref = rows_of_sibling(c, Y - k)
        return remote(ref, ref, ss_g.at[c, k], rs_g.at[c, k], (me, sibling))

    def arrive(c):
        for k in range(NSEQ - 1):
            got_a(c, k).wait_recv()
        inbox[...] = rv_a[c]
        cols = pl.ds(pl.multiple_of(c * CC, 128), CC)
        for r in range(RCAP):
            one = pl.ds(clips[r], 1)
            rows = inbox[srcs[r]].astype(F32)
            shaped = rows * (1.0 + md[1, one, cols]) + md[0, one, cols]
            gath[c, group, r * BLOCK : (r + 1) * BLOCK, :] = shaped.astype(BF16)
        for k in (2, 1, 3):
            send_b(c, k).start()
        send_g(c, 0).start()

    def forward(c):
        for k in (1, 3, 2):
            got_b(c, k).wait_recv()
            send_g(c, k).start()

    def project(c):
        for k in range(Y):
            got_g(c, k).wait_recv()
        at = pl.ds(pl.multiple_of(c * CC, 128), CC)

        def tile(n, carry):
            left = gath[c].reshape(ALL, CC)
            acc[n] += jnp.dot(left, win[n, at, :], preferred_element_type=F32)
            return carry

        lax.fori_loop(0, 6, tile, 0)

    for i in (0, 3, 4, 5):
        loads[i].wait()

    def first_half(t, carry):
        @pl.when(t < NC)
        def _():
            arrive(t)

        @pl.when(jnp.logical_and(t >= 1, t < NC + 1))
        def _():
            forward(t - 1)

        @pl.when(t >= 2)
        def _():
            project(t - 2)

        return carry

    lax.fori_loop(0, NC + 2, first_half, 0)

    def rms(v):
        return v * lax.rsqrt(jnp.mean(v * v, axis=-1, keepdims=True) + EPSILON)

    def shape_rows(b, carry):
        at = pl.ds(pl.multiple_of(b * ROWS, BLOCK), ROWS)
        for i in range(2):
            part = slice(i * HD, (i + 1) * HD)
            qa[i, at, 0:HD] = rms(acc[0, at, part]).astype(BF16)
            ka[i, at, 0:HD] = rms(acc[1, at, part]).astype(BF16)
            va[i, at, 0:HD] = acc[2, at, part].astype(BF16)
        for n in range(3):
            v = acc[3 + n, at, :]
            inner = 0.7978845608 * (v + 0.044715 * (v * v * v))
            ah[at, ATT + n * TILE : ATT + (n + 1) * TILE] = (
                0.5 * v * (1.0 + jnp.tanh(inner))
            ).astype(BF16)
        return carry

    lax.fori_loop(0, NHEAD, shape_rows, 0)

    def attend(b, carry):
        at = pl.ds(pl.multiple_of(b * QT, QT), QT)
        for i in range(2):
            scores = lax.dot_general(
                qa[i, at, :], ka[i], (((1,), (1,)), ((), ())), preferred_element_type=F32
            )
            powers = jnp.exp2(scores * EXP_A - EXP_B).astype(BF16)
            mixed = jnp.dot(powers, va[i], preferred_element_type=F32)
            ah[at, i * HD : (i + 1) * HD] = (mixed[:, 0:HD] / mixed[:, HD:]).astype(BF16)
        return carry

    lax.fori_loop(0, ALL // QT, attend, 0)

    for i in (1, 2):
        loads[i].wait()

    def send_s(c):
        return remote(term.at[c, 1 - core], rv_s.at[c], ss_s.at[c], rs_s.at[c], (me, sibling))

    def part(c, dy, half):
        return term.at[c, core, (y + dy) % Y, pl.ds(half * HALF, HALF)]

    def send_f(c, i):
        return remote(
            part(c, 2, i), rv_f.at[c, i], ss_f.at[c, i], rs_f.at[c, i],
            (me, head_at(1 if i == 0 else 3)),
        )

    def send_n(c, i, half):
        dy = 1 if i == 0 else 3
        return remote(
            part(c, dy, half), rv_n.at[c, i, pl.ds(half * HALF, HALF)],
            ss_n.at[c, 2 * i + half], rs_n.at[c, 2 * i + half], (me, head_at(dy)),
        )

    def out_project(c):
        for side in range(2):
            p = 1 - core if side == 0 else core

            def tile(n, carry):
                at = pl.ds(pl.multiple_of(c * CC + n * TILE, TILE), TILE)
                left = ah[pl.ds(pl.multiple_of(p * (ALL // 2), BLOCK), ALL // 2), :]
                got = jnp.dot(left, wo[:, at], preferred_element_type=F32).astype(BF16)
                to = pl.ds(pl.multiple_of(n * TILE, TILE), TILE)
                term[c, p, :, :, to] = got.reshape(Y, ROWS, TILE)
                return carry

            lax.fori_loop(0, NT, tile, 0)
            if side == 0:
                send_s(c).start()

    def pair_sum(c):
        send_s(c).wait_recv()

        def add(i, carry):
            term[c, core, i] = (term[c, core, i].astype(F32) + rv_s[c, i].astype(F32)).astype(BF16)
            return carry

        lax.fori_loop(0, Y, add, 0)
        send_f(c, 0).start()
        send_f(c, 1).start()
        send_n(c, 0, 1).start()
        send_n(c, 1, 0).start()

    def relay(c):
        for i in range(2):
            send_f(c, i).wait_recv()
            ref = part(c, 1 if i == 0 else 3, i)
            ref[...] = (ref[...].astype(F32) + rv_f[c, i].astype(F32)).astype(BF16)
            send_n(c, i, i).start()

    def send_e(c, k):
        to = seq_at(*OFFSETS[k])
        return remote(st_e.at[c, to], rv_e.at[c, me], ss_e.at[c, k], rs_e.at[c, k], (to, head))

    def got_e(c, k):
        dz, dx = OFFSETS[k]
        frm = seq_at(Z - dz, X - dx)
        return remote(st_e.at[c, frm], rv_e.at[c, frm], ss_e.at[c, k], rs_e.at[c, k], (frm, head))

    def finish(c):
        for i in range(2):
            for half in range(2):
                send_n(c, i, half).wait_recv()
        cols = pl.ds(pl.multiple_of(c * CC, 128), CC)
        for r in range(RCAP):
            at = slice(r * BLOCK, (r + 1) * BLOCK)
            total = (
                term[c, core, y, at, :].astype(F32)
                + rv_n[c, 0, at, :].astype(F32)
                + rv_n[c, 1, at, :].astype(F32)
            )
            fin[c, r] = (total * md[2, pl.ds(clips[r], 1), cols]).astype(BF16)

        def stage_back(t, carry):
            st_e[c, t] = fin[c, ranks[t]]
            return carry

        lax.fori_loop(0, NSEQ, stage_back, 0)
        for k in range(NSEQ - 1):
            send_e(c, k).start()
        rv_e[c, me] = st_e[c, me]

    def second_half(t, carry):
        @pl.when(t < NC)
        def _():
            out_project(t)

        @pl.when(jnp.logical_and(t >= 1, t < NC + 1))
        def _():
            pair_sum(t - 1)

        @pl.when(jnp.logical_and(t >= 2, t < NC + 2))
        def _():
            relay(t - 2)

        @pl.when(t >= 3)
        def _():
            finish(t - 3)

        return carry

    lax.fori_loop(0, NC + 3, second_half, 0)

    def collect(c, carry):
        for k in range(NSEQ - 1):
            got_e(c, k).wait_recv()
        inbox[...] = rv_e[c]
        cols = pl.ds(pl.multiple_of(c * CC, 128), CC)
        for j in range(BLK_DEV):
            at = slice(j * BLOCK, (j + 1) * BLOCK)
            back = inbox[targets[j]].astype(F32)
            out[at, cols] = (tok[at, cols].astype(F32) + back).astype(BF16)
        return carry

    lax.fori_loop(0, NC, collect, 0)

    def drain(c, carry):
        for k in range(NSEQ - 1):
            send_a(c, k).wait_send()
            send_e(c, k).wait_send()
        for k in range(1, Y):
            send_b(c, k).wait_send()
        for k in range(Y):
            send_g(c, k).wait_send()
        send_s(c).wait_send()
        for i in range(2):
            send_f(c, i).wait_send()
            for half in range(2):
                send_n(c, i, half).wait_send()
        return carry

    lax.fori_loop(0, NC, drain, 0)


def body(
    tokens, block_target, clip_within, modulation,
    inner_attention, inner_hidden, outer_attention, outer_hidden,
):
    smem = pl.BlockSpec(memory_space=pltpu.SMEM)
    vmem = pl.BlockSpec(memory_space=pltpu.VMEM)
    anywhere = pl.BlockSpec(memory_space=pl.ANY)
    dma = pltpu.SemaphoreType.DMA
    return pl.pallas_call(
        kernel,
        out_shape=jax.ShapeDtypeStruct((BLK_DEV * BLOCK, D), BF16),
        in_specs=[smem, smem, vmem, vmem, anywhere, anywhere, anywhere, anywhere],
        out_specs=vmem,
        scratch_shapes=[
            pltpu.VMEM((BLK_DEV, BLOCK, D), BF16),
            pltpu.VMEM((NSEQ, BLOCK, CC), BF16),
            pltpu.VMEM((NC, NSEQ, BLOCK, CC), BF16),
            pltpu.VMEM((NC, NSEQ, BLOCK, CC), BF16),
            pltpu.VMEM((NC, NHEAD, ROWS, CC), BF16),
            pltpu.VMEM((6, D, TILE), BF16),
            pltpu.VMEM((ATT + HID, D), BF16),
            pltpu.VMEM((6, ALL, TILE), F32),
            pltpu.VMEM((2, ALL, 2 * HD), BF16),
            pltpu.VMEM((2, ALL, 2 * HD), BF16),
            pltpu.VMEM((2, ALL, 2 * HD), BF16),
            pltpu.VMEM((ALL, ATT + HID), BF16),
            pltpu.VMEM((NC, 2, Y, ROWS, CC), BF16),
            pltpu.VMEM((NC, Y, ROWS, CC), BF16),
            pltpu.VMEM((NC, 2, HALF, CC), BF16),
            pltpu.VMEM((NC, 2, ROWS, CC), BF16),
            pltpu.VMEM((NC, RCAP, BLOCK, CC), BF16),
            pltpu.VMEM((NC, NSEQ, BLOCK, CC), BF16),
            pltpu.VMEM((NC, NSEQ, BLOCK, CC), BF16),
            pltpu.SMEM((NSEQ,), jnp.int32),
            pltpu.SMEM((RCAP,), jnp.int32),
            pltpu.SMEM((RCAP,), jnp.int32),
            dma((6,)),
            dma((NC, NSEQ)), dma((NC, NSEQ)),
            dma((NC, Y)), dma((NC, Y)),
            dma((NC, Y)), dma((NC, Y)),
            dma((NC,)), dma((NC,)),
            dma((NC, 2)), dma((NC, 2)),
            dma((NC, 4)), dma((NC, 4)),
            dma((NC, NSEQ)), dma((NC, NSEQ)),
        ],
        compiler_params=pltpu.CompilerParams(
            collective_id=0, has_side_effects=True, vmem_limit_bytes=62 << 20
        ),
        cost_estimate=pl.CostEstimate(
            flops=13_000_000_000, bytes_accessed=17_000_000, transcendentals=2_000_000
        ),
    )(
        block_target, clip_within, tokens, jnp.transpose(modulation, (1, 0, 2)),
        jnp.transpose(inner_attention, (1, 0, 2)), inner_hidden, outer_attention, outer_hidden,
    )


def solution(mesh):
    placed = (
        P(("seq", "head"), None),
        P(),
        P(),
        P("seq", None, None),
        P(None, None, "head"),
        P(None, "head"),
        P("head", None),
        P("head", None),
    )
    return jax.shard_map(
        body, mesh=mesh, in_specs=placed, out_specs=P(("seq", "head"), None), check_vma=False
    )
```

time: 330 us -> 93 us (0.28)
  waiting for transfers between devices: 203 us -> 0 us
  Pallas kernels: 0 us -> 91.1 us
  matrix products: 33.4 us -> 0 us
  other arithmetic: 30.4 us -> 0 us
  local copies, waits for them, and re-layouts: 29 us -> 1.77 us
  starting transfers between devices: 18.5 us -> 0 us
  between operations: 13.8 us -> 0.01 us
    all_to_all x2 -> x0, waiting for transfers between devices: 161 us -> none  [the longest x1 140 us: body(): lax.all_to_all(fanned, ('seq', 'head'), split_axis=0, concat_axis=0, tile...]
    pallas_call x0 -> x1, Pallas kernels: none -> 91.1 us  [body(): pl.pallas_call(kernel, out_shape=jax.ShapeDtypeStruct((BLK_DEV * BLOCK, D...]
    reduce_scatter x1 -> x0, waiting for transfers between devices: 42.1 us -> none  [body(): lax.psum_scatter((first + jnp.dot(hidden, outer_hidden, preferred_element...]
    dot_general x5 -> x0, matrix products: 33.4 us -> none  [the longest x1 16.5 us: body(): jnp.dot(hidden, outer_hidden, preferred_element_type=jnp.float32)]
    all_to_all x2 -> x0, starting transfers between devices: 18.5 us -> none  [the longest x1 11.6 us: body(): lax.all_to_all(fanned, ('seq', 'head'), split_axis=0, concat_axis=0, tile...]
    gather x4 -> x0, local copies, waits for them, and re-layouts: 12.9 us -> none  [the longest x1 7.68 us: body(): group_rows = jnp.take(received, flat_index.reshape(-1), axis=0)]
    convert_element_type x6 -> x0, other arithmetic: 11.7 us -> none  [the longest x2 10.1 us: modulate(): return (shaped.astype(jnp.bfloat16), picked[:, 2])]
    reduce_sum x7 -> x0, other arithmetic: 11 us -> none  [the longest x1 5.93 us: layer_norm(): centred = values - jnp.mean(values, axis=-1, keepdims=True)]
  transfers between devices with their start and end apart: 3 -> 0, of which waited for: 3 -> 0; matrix products, arithmetic and copies ran while one was open for 4% -> 0% of each run, Pallas kernels for 0% -> 0%
where the time goes in v1:
time: 93 us; the launch traced here: 92.9 us
  Pallas kernels  91.1 us (98%)
  local copies, waits for them, and re-layouts  1.77 us (2%)
    pallas_call x1, Pallas kernels, body(): pl.pallas_call(kernel, out_shape=jax.ShapeDtypeStruct((BLK_DEV * BLOCK, D...  91.1 us

profile of v1, /device:TPU:0, one launch (start us, length us, event | category | flops | bytes accessed | tf_op | source)
XLA Modules:
  0.0 92.9 jit_solution(9927045911594436833)
XLA Ops:
  0.0 91.1 %shard_map.82 = bf16[64,3072]{1,0:T(8,128)(2,1)} custom-call(s32[512]{0:T(512)} %bt.1, s32[512]{0:T(512)} %cw.1, bf16[64,3072]{1,0:T(8,128)(2,1)} %tok.1, f32[3,4,3072]{2,1,0:T(4,128)} %bitcast.3, bf16[3,3072,256]{2,1,0:T(8,128)(2,1)} %bitcast.2, bf16[3072,768]{1,0:T(8,128)(2,1)} %wh.1, bf16[256,3072]{1,0:T(8,128)(2,1)} %woa.1, bf16[768,3072]{1,0:T(8,128)(2,1)} %woh.1), custom_call_target="tpu_custom_call" | custom-call | flops 12999999488 | bytes 17000000 | tf_op jit(solution)/shard_map/pallas_call | solution.py:439
  91.1 1.8 %copy.10 = bf16[64,3072]{1,0:T(8,128)(2,1)} copy(bf16[64,3072]{1,0:T(8,128)(2,1)} %shard_map.82) | data formatting | bytes 786432

commit v2 on v1

--- a/solution.py
+++ b/solution.py
@@ -27,13 +27,15 @@
 ROWS = RCAP * BLOCK
 ALL = NHEAD * ROWS
 HALF = ROWS // 2
-NC = 4
+NC = 6
 CC = D // NC
-TILE = 256
 QT = 256
-NT = CC // TILE
 ATT = 256
 HID = 768
+PEERS = NSEQ - 1
+AHEAD = 2
+LAG_B = (1, 2, 3)
+LAG_D = (1, 2, 3)
 BIG = 1536.0
 EXP_A = HD ** (-0.5) * math.log2(math.e)
 EXP_B = BIG * EXP_A
@@ -48,8 +50,8 @@
     bt, cw, tok, md, wq, wh, woa, woh, out,
     nrm, inbox, st_a, rv_a, gath, win, wo, acc, qa, ka, va, ah,
     term, rv_s, rv_f, rv_n, fin, st_e, rv_e, ranks, srcs, clips,
-    w_sem, ss_a, rs_a, ss_b, rs_b, ss_g, rs_g,
-    ss_s, rs_s, ss_f, rs_f, ss_n, rs_n, ss_e, rs_e,
+    w_sem, ss_a, rs_a, ss_b, rs_b, rs_g,
+    ss_d, rs_s, rs_f, rs_n, ss_e, rs_e,
 ):
     me = lax.axis_index("seq")
     head = lax.axis_index("head")
@@ -64,18 +66,24 @@
     def head_at(dy):
         return ((y + dy) % Y) * 2 + core
 
+    def arrived(ref, sem):
+        remote(ref, ref, sem, sem, (me, sibling)).wait_recv()
+
+    def left(ref, sem):
+        remote(ref, ref, sem, sem, (me, sibling)).wait_send()
+
     def remote(src, dst, ss, rs, dev):
         return pltpu.make_async_remote_copy(
             src_ref=src, dst_ref=dst, send_sem=ss, recv_sem=rs, device_id=dev, device_id_type=MESH
         )
 
     loads = [
-        pltpu.make_async_copy(wq, win.at[pl.ds(0, 3)], w_sem.at[0]),
-        pltpu.make_async_copy(woa, wo.at[pl.ds(0, ATT)], w_sem.at[1]),
-        pltpu.make_async_copy(woh, wo.at[pl.ds(ATT, HID)], w_sem.at[2]),
+        pltpu.make_async_copy(wq.at[n], win.at[0, :, pl.ds(n * ATT, ATT)], w_sem.at[n])
+        for n in range(3)
     ] + [
-        pltpu.make_async_copy(wh.at[:, pl.ds(n * TILE, TILE)], win.at[3 + n], w_sem.at[3 + n])
-        for n in range(3)
+        pltpu.make_async_copy(wh, win.at[1], w_sem.at[3]),
+        pltpu.make_async_copy(woa, wo.at[pl.ds(0, ATT)], w_sem.at[4]),
+        pltpu.make_async_copy(woh, wo.at[pl.ds(ATT, HID)], w_sem.at[5]),
     ]
     for load in loads:
         load.start()
@@ -109,20 +117,15 @@
 
     def send_a(c, k):
         to = seq_at(*OFFSETS[k])
-        return remote(st_a.at[c, to], rv_a.at[c, me], ss_a.at[c, k], rs_a.at[c, k], (to, head))
-
-    def got_a(c, k):
-        dz, dx = OFFSETS[k]
-        frm = seq_at(Z - dz, X - dx)
-        return remote(st_a.at[c, frm], rv_a.at[c, frm], ss_a.at[c, k], rs_a.at[c, k], (frm, head))
-
-    def start_a(c, carry):
-        for k in range(NSEQ - 1):
+        return remote(st_a.at[c, to], rv_a.at[c, me], ss_a.at[c], rs_a.at[c], (to, head))
+
+    def start_a(c):
+        for k in range(PEERS):
             send_a(c, k).start()
         rv_a[c, me] = st_a[c, me]
-        return carry
-
-    lax.fori_loop(0, NC, start_a, 0)
+
+    for c in range(AHEAD):
+        start_a(c)
 
     def entry(s, h):
         live, clip = jnp.int32(0), jnp.int32(0)
@@ -173,10 +176,10 @@
     lax.fori_loop(0, NHEAD, group_slots, 0)
 
     def clear(n, carry):
-        acc[n] = jnp.zeros((ALL, TILE), F32)
-        return carry
-
-    lax.fori_loop(0, 6, clear, 0)
+        acc[n] = jnp.zeros((ALL, HID), F32)
+        return carry
+
+    lax.fori_loop(0, 2, clear, 0)
 
     def own_rows(c):
         return gath.at[c, group]
@@ -184,27 +187,24 @@
     def rows_of(c, dy):
         return gath.at[c, core * Y + (y + dy) % Y]
 
-    def rows_of_sibling(c, dy):
-        return gath.at[c, (1 - core) * Y + (y + dy) % Y]
-
     def send_b(c, k):
-        return remote(own_rows(c), own_rows(c), ss_b.at[c, k], rs_b.at[c, k], (me, head_at(k)))
-
-    def got_b(c, k):
-        ref = rows_of(c, Y - k)
-        return remote(ref, ref, ss_b.at[c, k], rs_b.at[c, k], (me, head_at(Y - k)))
-
-    def send_g(c, k):
-        ref = rows_of(c, Y - k)
-        return remote(ref, ref, ss_g.at[c, k], rs_g.at[c, k], (me, sibling))
-
-    def got_g(c, k):
-        ref = rows_of_sibling(c, Y - k)
-        return remote(ref, ref, ss_g.at[c, k], rs_g.at[c, k], (me, sibling))
+        return remote(own_rows(c), own_rows(c), ss_b.at[c], rs_b.at[c, k // 2], (me, head_at(k)))
+
+    def pass_b(c, k):
+        ref = rows_of(c, Y - k).at[pl.ds((k // 2) * HALF, HALF)]
+        return remote(ref, ref, ss_b.at[c], rs_b.at[c, 2], (me, head_at(k)))
+
+    def send_g(c, dy):
+        ref = rows_of(c, dy)
+        return remote(ref, ref, ss_b.at[c], rs_g.at[c], (me, sibling))
 
     def arrive(c):
-        for k in range(NSEQ - 1):
-            got_a(c, k).wait_recv()
+        arrived(rv_a.at[c, pl.ds(0, PEERS)], rs_a.at[c])
+
+        @pl.when(c + AHEAD < NC)
+        def _():
+            start_a(c + AHEAD)
+
         inbox[...] = rv_a[c]
         cols = pl.ds(pl.multiple_of(c * CC, 128), CC)
         for r in range(RCAP):
@@ -212,28 +212,32 @@
             rows = inbox[srcs[r]].astype(F32)
             shaped = rows * (1.0 + md[1, one, cols]) + md[0, one, cols]
             gath[c, group, r * BLOCK : (r + 1) * BLOCK, :] = shaped.astype(BF16)
-        for k in (2, 1, 3):
+        for k in (1, 3):
             send_b(c, k).start()
         send_g(c, 0).start()
 
-    def forward(c):
-        for k in (1, 3, 2):
-            got_b(c, k).wait_recv()
-            send_g(c, k).start()
+    def forward_near(c):
+        for k in (1, 3):
+            arrived(rows_of(c, Y - k), rs_b.at[c, k // 2])
+            pass_b(c, k).start()
+            send_g(c, Y - k).start()
+
+    def forward_far(c):
+        arrived(rows_of(c, 2), rs_b.at[c, 2])
+        send_g(c, 2).start()
 
     def project(c):
-        for k in range(Y):
-            got_g(c, k).wait_recv()
+        arrived(gath.at[c, pl.ds((1 - core) * Y, Y)], rs_g.at[c])
         at = pl.ds(pl.multiple_of(c * CC, 128), CC)
 
         def tile(n, carry):
-            left = gath[c].reshape(ALL, CC)
-            acc[n] += jnp.dot(left, win[n, at, :], preferred_element_type=F32)
+            rows = gath[c].reshape(ALL, CC)
+            acc[n] += jnp.dot(rows, win[n, at, :], preferred_element_type=F32)
             return carry
 
-        lax.fori_loop(0, 6, tile, 0)
-
-    for i in (0, 3, 4, 5):
+        lax.fori_loop(0, 2, tile, 0)
+
+    for i in range(4):
         loads[i].wait()
 
     def first_half(t, carry):
@@ -241,17 +245,15 @@
         def _():
             arrive(t)
 
-        @pl.when(jnp.logical_and(t >= 1, t < NC + 1))
-        def _():
-            forward(t - 1)
-
-        @pl.when(t >= 2)
-        def _():
-            project(t - 2)
-
-        return carry
-
-    lax.fori_loop(0, NC + 2, first_half, 0)
+        for lag, step in zip(LAG_B, (forward_near, forward_far, project), strict=True):
+
+            @pl.when(jnp.logical_and(t >= lag, t < NC + lag))
+            def _(lag=lag, step=step):
+                step(t - lag)
+
+        return carry
+
+    lax.fori_loop(0, NC + LAG_B[-1], first_half, 0)
 
     def rms(v):
         return v * lax.rsqrt(jnp.mean(v * v, axis=-1, keepdims=True) + EPSILON)
@@ -259,16 +261,13 @@
     def shape_rows(b, carry):
         at = pl.ds(pl.multiple_of(b * ROWS, BLOCK), ROWS)
         for i in range(2):
-            part = slice(i * HD, (i + 1) * HD)
-            qa[i, at, 0:HD] = rms(acc[0, at, part]).astype(BF16)
-            ka[i, at, 0:HD] = rms(acc[1, at, part]).astype(BF16)
-            va[i, at, 0:HD] = acc[2, at, part].astype(BF16)
-        for n in range(3):
-            v = acc[3 + n, at, :]
-            inner = 0.7978845608 * (v + 0.044715 * (v * v * v))
-            ah[at, ATT + n * TILE : ATT + (n + 1) * TILE] = (
-                0.5 * v * (1.0 + jnp.tanh(inner))
-            ).astype(BF16)
+            part = [slice(n * ATT + i * HD, n * ATT + (i + 1) * HD) for n in range(3)]
+            qa[i, at, 0:HD] = rms(acc[0, at, part[0]]).astype(BF16)
+            ka[i, at, 0:HD] = rms(acc[0, at, part[1]]).astype(BF16)
+            va[i, at, 0:HD] = acc[0, at, part[2]].astype(BF16)
+        v = acc[1, at, :]
+        inner = 0.7978845608 * (v + 0.044715 * (v * v * v))
+        ah[at, ATT:] = (0.5 * v * (1.0 + jnp.tanh(inner))).astype(BF16)
         return carry
 
     lax.fori_loop(0, NHEAD, shape_rows, 0)
@@ -286,18 +285,18 @@
 
     lax.fori_loop(0, ALL // QT, attend, 0)
 
-    for i in (1, 2):
+    for i in (4, 5):
         loads[i].wait()
 
     def send_s(c):
-        return remote(term.at[c, 1 - core], rv_s.at[c], ss_s.at[c], rs_s.at[c], (me, sibling))
+        return remote(term.at[c, 1 - core], rv_s.at[c], ss_d.at[c], rs_s.at[c], (me, sibling))
 
     def part(c, dy, half):
         return term.at[c, core, (y + dy) % Y, pl.ds(half * HALF, HALF)]
 
     def send_f(c, i):
         return remote(
-            part(c, 2, i), rv_f.at[c, i], ss_f.at[c, i], rs_f.at[c, i],
+            part(c, 2, i), rv_f.at[c, i], ss_d.at[c], rs_f.at[c, i],
             (me, head_at(1 if i == 0 else 3)),
         )
 
@@ -305,22 +304,17 @@
         dy = 1 if i == 0 else 3
         return remote(
             part(c, dy, half), rv_n.at[c, i, pl.ds(half * HALF, HALF)],
-            ss_n.at[c, 2 * i + half], rs_n.at[c, 2 * i + half], (me, head_at(dy)),
+            ss_d.at[c], rs_n.at[c], (me, head_at(dy)),
         )
 
     def out_project(c):
         for side in range(2):
             p = 1 - core if side == 0 else core
 
-            def tile(n, carry):
-                at = pl.ds(pl.multiple_of(c * CC + n * TILE, TILE), TILE)
-                left = ah[pl.ds(pl.multiple_of(p * (ALL // 2), BLOCK), ALL // 2), :]
-                got = jnp.dot(left, wo[:, at], preferred_element_type=F32).astype(BF16)
-                to = pl.ds(pl.multiple_of(n * TILE, TILE), TILE)
-                term[c, p, :, :, to] = got.reshape(Y, ROWS, TILE)
-                return carry
-
-            lax.fori_loop(0, NT, tile, 0)
+            at = pl.ds(pl.multiple_of(c * CC, 128), CC)
+            rows = ah[pl.ds(pl.multiple_of(p * (ALL // 2), BLOCK), ALL // 2), :]
+            got = jnp.dot(rows, wo[:, at], preferred_element_type=F32).astype(BF16)
+            term[c, p] = got.reshape(Y, ROWS, CC)
             if side == 0:
                 send_s(c).start()
 
@@ -346,17 +340,10 @@
 
     def send_e(c, k):
         to = seq_at(*OFFSETS[k])
-        return remote(st_e.at[c, to], rv_e.at[c, me], ss_e.at[c, k], rs_e.at[c, k], (to, head))
-
-    def got_e(c, k):
-        dz, dx = OFFSETS[k]
-        frm = seq_at(Z - dz, X - dx)
-        return remote(st_e.at[c, frm], rv_e.at[c, frm], ss_e.at[c, k], rs_e.at[c, k], (frm, head))
+        return remote(st_e.at[c, to], rv_e.at[c, me], ss_e.at[c], rs_e.at[c], (to, head))
 
     def finish(c):
-        for i in range(2):
-            for half in range(2):
-                send_n(c, i, half).wait_recv()
+        arrived(rv_n.at[c], rs_n.at[c])
         cols = pl.ds(pl.multiple_of(c * CC, 128), CC)
         for r in range(RCAP):
             at = slice(r * BLOCK, (r + 1) * BLOCK)
@@ -372,7 +359,7 @@
             return carry
 
         lax.fori_loop(0, NSEQ, stage_back, 0)
-        for k in range(NSEQ - 1):
+        for k in range(PEERS):
             send_e(c, k).start()
         rv_e[c, me] = st_e[c, me]
 
@@ -381,25 +368,18 @@
         def _():
             out_project(t)
 
-        @pl.when(jnp.logical_and(t >= 1, t < NC + 1))
-        def _():
-            pair_sum(t - 1)
-
-        @pl.when(jnp.logical_and(t >= 2, t < NC + 2))
-        def _():
-            relay(t - 2)
-
-        @pl.when(t >= 3)
-        def _():
-            finish(t - 3)
-
-        return carry
-
-    lax.fori_loop(0, NC + 3, second_half, 0)
+        for lag, step in zip(LAG_D, (pair_sum, relay, finish), strict=True):
+
+            @pl.when(jnp.logical_and(t >= lag, t < NC + lag))
+            def _(lag=lag, step=step):
+                step(t - lag)
+
+        return carry
+
+    lax.fori_loop(0, NC + LAG_D[-1], second_half, 0)
 
     def collect(c, carry):
-        for k in range(NSEQ - 1):
-            got_e(c, k).wait_recv()
+        arrived(rv_e.at[c, pl.ds(0, PEERS)], rs_e.at[c])
         inbox[...] = rv_e[c]
         cols = pl.ds(pl.multiple_of(c * CC, 128), CC)
         for j in range(BLK_DEV):
@@ -411,18 +391,10 @@
     lax.fori_loop(0, NC, collect, 0)
 
     def drain(c, carry):
-        for k in range(NSEQ - 1):
-            send_a(c, k).wait_send()
-            send_e(c, k).wait_send()
-        for k in range(1, Y):
-            send_b(c, k).wait_send()
-        for k in range(Y):
-            send_g(c, k).wait_send()
-        send_s(c).wait_send()
-        for i in range(2):
-            send_f(c, i).wait_send()
-            for half in range(2):
-                send_n(c, i, half).wait_send()
+        left(st_a.at[c, pl.ds(0, PEERS)], ss_a.at[c])
+        left(st_e.at[c, pl.ds(0, PEERS)], ss_e.at[c])
+        left(gath.at[c, pl.ds(0, 7)], ss_b.at[c])
+        left(gath.at[c, pl.ds(0, 7)], ss_d.at[c])
         return carry
 
     lax.fori_loop(0, NC, drain, 0)
@@ -447,9 +419,9 @@
             pltpu.VMEM((NC, NSEQ, BLOCK, CC), BF16),
             pltpu.VMEM((NC, NSEQ, BLOCK, CC), BF16),
             pltpu.VMEM((NC, NHEAD, ROWS, CC), BF16),
-            pltpu.VMEM((6, D, TILE), BF16),
+            pltpu.VMEM((2, D, HID), BF16),
             pltpu.VMEM((ATT + HID, D), BF16),
-            pltpu.VMEM((6, ALL, TILE), F32),
+            pltpu.VMEM((2, ALL, HID), F32),
             pltpu.VMEM((2, ALL, 2 * HD), BF16),
             pltpu.VMEM((2, ALL, 2 * HD), BF16),
             pltpu.VMEM((2, ALL, 2 * HD), BF16),
@@ -465,13 +437,10 @@
             pltpu.SMEM((RCAP,), jnp.int32),
             pltpu.SMEM((RCAP,), jnp.int32),
             dma((6,)),
-            dma((NC, NSEQ)), dma((NC, NSEQ)),
-            dma((NC, Y)), dma((NC, Y)),
-            dma((NC, Y)), dma((NC, Y)),
             dma((NC,)), dma((NC,)),
-            dma((NC, 2)), dma((NC, 2)),
-            dma((NC, 4)), dma((NC, 4)),
-            dma((NC, NSEQ)), dma((NC, NSEQ)),
+            dma((NC,)), dma((NC, Y - 1)), dma((NC,)),
+            dma((NC,)), dma((NC,)), dma((NC, 2)), dma((NC,)),
+            dma((NC,)), dma((NC,)),
         ],
         compiler_params=pltpu.CompilerParams(
             collective_id=0, has_side_effects=True, vmem_limit_bytes=62 << 20

time: 93 us -> 84.3 us (0.906)
  Pallas kernels: 91.1 us -> 82.4 us
    pallas_call x1, Pallas kernels: 91.1 us -> 82.4 us  [body(): pl.pallas_call(kernel, out_shape=jax.ShapeDtypeStruct((BLK_DEV * BLOCK, D...]
where the time goes in v2:
time: 84.3 us; the launch traced here: 84.2 us
  Pallas kernels  82.4 us (98%)
  local copies, waits for them, and re-layouts  1.77 us (2%)
    pallas_call x1, Pallas kernels, body(): pl.pallas_call(kernel, out_shape=jax.ShapeDtypeStruct((BLK_DEV * BLOCK, D...  82.4 us
    unnamed x1, local copies, waits for them, and re-layouts  1.77 us

profile of v2, /device:TPU:0, one launch (start us, length us, event | category | flops | bytes accessed | tf_op | source)
XLA Modules:
  0.0 84.2 jit_solution(3860656084786691867)
XLA Ops:
  0.0 82.4 %shard_map.82 = bf16[64,3072]{1,0:T(8,128)(2,1)} custom-call(s32[512]{0:T(512)} %bt.1, s32[512]{0:T(512)} %cw.1, bf16[64,3072]{1,0:T(8,128)(2,1)} %tok.1, f32[3,4,3072]{2,1,0:T(4,128)} %bitcast.3, bf16[3,3072,256]{2,1,0:T(8,128)(2,1)} %bitcast.2, bf16[3072,768]{1,0:T(8,128)(2,1)} %wh.1, bf16[256,3072]{1,0:T(8,128)(2,1)} %woa.1, bf16[768,3072]{1,0:T(8,128)(2,1)} %woh.1), custom_call_target="tpu_custom_call" | custom-call | flops 12999999488 | bytes 17000000 | tf_op jit(solution)/shard_map/pallas_call | solution.py:411
  82.4 1.8 %copy.10 = bf16[64,3072]{1,0:T(8,128)(2,1)} copy(bf16[64,3072]{1,0:T(8,128)(2,1)} %shard_map.82) | data formatting | bytes 786432

commit v3 on v2

--- a/solution.py
+++ b/solution.py
@@ -29,12 +29,16 @@
 HALF = ROWS // 2
 NC = 6
 CC = D // NC
-QT = 256
+ND = 6
+CD = D // ND
+QT = ALL // 2
 ATT = 256
 HID = 768
 PEERS = NSEQ - 1
-AHEAD = 2
-LAG_B = (1, 2, 3)
+SLOT = {0: 0, 1: 1, 3: 2, 2: 3}
+NEAR = 6
+AHEAD = 3
+LAG_B = (1, 3, 2)
 LAG_D = (1, 2, 3)
 BIG = 1536.0
 EXP_A = HD ** (-0.5) * math.log2(math.e)
@@ -48,7 +52,7 @@
 
 def kernel(
     bt, cw, tok, md, wq, wh, woa, woh, out,
-    nrm, inbox, st_a, rv_a, gath, win, wo, acc, qa, ka, va, ah,
+    nrm, inbox, outbox, st_a, rv_a, gath, win, wo, acc, qa, ka, va, ah,
     term, rv_s, rv_f, rv_n, fin, st_e, rv_e, ranks, srcs, clips,
     w_sem, ss_a, rs_a, ss_b, rs_b, rs_g,
     ss_d, rs_s, rs_f, rs_n, ss_e, rs_e,
@@ -58,7 +62,6 @@
     z, x = me // X, me % X
     y, core = head // 2, head % 2
     sibling = head + 1 - 2 * core
-    group = core * Y + y
 
     def seq_at(dz, dx):
         return ((z + dz) % Z) * X + (x + dx) % X
@@ -154,7 +157,9 @@
     lanes = lax.broadcasted_iota(jnp.int32, (BLOCK, HD), 1)
 
     def group_slots(g, carry):
-        h = (g % Y) * 2 + g // Y
+        place = g // 2
+        dy = place + place // 2 - 2 * (place // 3)
+        h = ((y + dy) % Y) * 2 + g % 2
 
         def slot(s, carry):
             count, named = carry
@@ -173,30 +178,28 @@
                 va[i, at, HD:] = jnp.ones((BLOCK, HD), BF16)
         return carry
 
-    lax.fori_loop(0, NHEAD, group_slots, 0)
-
     def clear(n, carry):
         acc[n] = jnp.zeros((ALL, HID), F32)
         return carry
 
     lax.fori_loop(0, 2, clear, 0)
 
-    def own_rows(c):
-        return gath.at[c, group]
-
-    def rows_of(c, dy):
-        return gath.at[c, core * Y + (y + dy) % Y]
-
     def send_b(c, k):
-        return remote(own_rows(c), own_rows(c), ss_b.at[c], rs_b.at[c, k // 2], (me, head_at(k)))
+        return remote(
+            gath.at[c, 0, core], gath.at[c, SLOT[Y - k], core],
+            ss_b.at[c, 0], rs_b.at[c, k // 2], (me, head_at(k)),
+        )
 
     def pass_b(c, k):
-        ref = rows_of(c, Y - k).at[pl.ds((k // 2) * HALF, HALF)]
-        return remote(ref, ref, ss_b.at[c], rs_b.at[c, 2], (me, head_at(k)))
-
-    def send_g(c, dy):
-        ref = rows_of(c, dy)
-        return remote(ref, ref, ss_b.at[c], rs_g.at[c], (me, sibling))
+        half = pl.ds((k // 2) * HALF, HALF)
+        return remote(
+            gath.at[c, SLOT[Y - k], core, half], gath.at[c, SLOT[2], core, half],
+            ss_b.at[c, 0], rs_b.at[c, 2], (me, head_at(k)),
+        )
+
+    def send_g(c, slot):
+        ref = gath.at[c, slot, core]
+        return remote(ref, ref, ss_b.at[c, 1], rs_g.at[c, slot // 3], (me, sibling))
 
     def arrive(c):
         arrived(rv_a.at[c, pl.ds(0, PEERS)], rs_a.at[c])
@@ -211,49 +214,33 @@
             one = pl.ds(clips[r], 1)
             rows = inbox[srcs[r]].astype(F32)
             shaped = rows * (1.0 + md[1, one, cols]) + md[0, one, cols]
-            gath[c, group, r * BLOCK : (r + 1) * BLOCK, :] = shaped.astype(BF16)
+            gath[c, 0, core, r * BLOCK : (r + 1) * BLOCK, :] = shaped.astype(BF16)
         for k in (1, 3):
             send_b(c, k).start()
         send_g(c, 0).start()
 
     def forward_near(c):
         for k in (1, 3):
-            arrived(rows_of(c, Y - k), rs_b.at[c, k // 2])
+            slot = SLOT[Y - k]
+            arrived(gath.at[c, slot, core], rs_b.at[c, k // 2])
             pass_b(c, k).start()
-            send_g(c, Y - k).start()
+            send_g(c, slot).start()
 
     def forward_far(c):
-        arrived(rows_of(c, 2), rs_b.at[c, 2])
-        send_g(c, 2).start()
-
-    def project(c):
-        arrived(gath.at[c, pl.ds((1 - core) * Y, Y)], rs_g.at[c])
+        arrived(gath.at[c, 3, core], rs_b.at[c, 2])
+        send_g(c, 3).start()
+
+    def project_rows(c, slots):
+        rows = len(slots) * 2 * ROWS
         at = pl.ds(pl.multiple_of(c * CC, 128), CC)
+        to = pl.ds(slots[0] * 2 * ROWS, rows)
 
         def tile(n, carry):
-            rows = gath[c].reshape(ALL, CC)
-            acc[n] += jnp.dot(rows, win[n, at, :], preferred_element_type=F32)
+            left = gath[c, slots[0] : slots[-1] + 1].reshape(rows, CC)
+            acc[n, to, :] += jnp.dot(left, win[n, at, :], preferred_element_type=F32)
             return carry
 
         lax.fori_loop(0, 2, tile, 0)
-
-    for i in range(4):
-        loads[i].wait()
-
-    def first_half(t, carry):
-        @pl.when(t < NC)
-        def _():
-            arrive(t)
-
-        for lag, step in zip(LAG_B, (forward_near, forward_far, project), strict=True):
-
-            @pl.when(jnp.logical_and(t >= lag, t < NC + lag))
-            def _(lag=lag, step=step):
-                step(t - lag)
-
-        return carry
-
-    lax.fori_loop(0, NC + LAG_B[-1], first_half, 0)
 
     def rms(v):
         return v * lax.rsqrt(jnp.mean(v * v, axis=-1, keepdims=True) + EPSILON)
@@ -267,10 +254,49 @@
             va[i, at, 0:HD] = acc[0, at, part[2]].astype(BF16)
         v = acc[1, at, :]
         inner = 0.7978845608 * (v + 0.044715 * (v * v * v))
-        ah[at, ATT:] = (0.5 * v * (1.0 + jnp.tanh(inner))).astype(BF16)
-        return carry
-
-    lax.fori_loop(0, NHEAD, shape_rows, 0)
+        ah[b // 2, b % 2, :, ATT:] = (0.5 * v * (1.0 + jnp.tanh(inner))).astype(BF16)
+        return carry
+
+    def project(c):
+        near = gath.at[c, pl.ds(0, 3), 1 - core]
+        far = gath.at[c, 3, 1 - core]
+
+        @pl.when(c < NC - 1)
+        def _():
+            arrived(near, rs_g.at[c, 0])
+            arrived(far, rs_g.at[c, 1])
+            project_rows(c, range(Y))
+
+        @pl.when(c == NC - 1)
+        def _():
+            arrived(near, rs_g.at[c, 0])
+            project_rows(c, range(3))
+            lax.fori_loop(0, NEAR, shape_rows, 0)
+            arrived(far, rs_g.at[c, 1])
+            project_rows(c, range(3, Y))
+            lax.fori_loop(NEAR, NHEAD, shape_rows, 0)
+
+    for i in range(4):
+        loads[i].wait()
+
+    def first_half(t, carry):
+        @pl.when(t < NC)
+        def _():
+            arrive(t)
+
+        @pl.when(t < NHEAD)
+        def _():
+            group_slots(t, 0)
+
+        for lag, step in zip(LAG_B, (forward_near, project, forward_far), strict=True):
+
+            @pl.when(jnp.logical_and(t >= lag, t < NC + lag))
+            def _(lag=lag, step=step):
+                step(t - lag)
+
+        return carry
+
+    lax.fori_loop(0, NC + max(LAG_B), first_half, 0)
 
     def attend(b, carry):
         at = pl.ds(pl.multiple_of(b * QT, QT), QT)
@@ -280,7 +306,8 @@
             )
             powers = jnp.exp2(scores * EXP_A - EXP_B).astype(BF16)
             mixed = jnp.dot(powers, va[i], preferred_element_type=F32)
-            ah[at, i * HD : (i + 1) * HD] = (mixed[:, 0:HD] / mixed[:, HD:]).astype(BF16)
+            found = (mixed[:, 0:HD] / mixed[:, HD:]).astype(BF16)
+            ah[pl.ds(b * 2, 2), :, :, i * HD : (i + 1) * HD] = found.reshape(2, 2, ROWS, HD)
         return carry
 
     lax.fori_loop(0, ALL // QT, attend, 0)
@@ -289,52 +316,54 @@
         loads[i].wait()
 
     def send_s(c):
-        return remote(term.at[c, 1 - core], rv_s.at[c], ss_d.at[c], rs_s.at[c], (me, sibling))
-
-    def part(c, dy, half):
-        return term.at[c, core, (y + dy) % Y, pl.ds(half * HALF, HALF)]
+        return remote(term.at[c, :, 1 - core], rv_s.at[c], ss_d.at[c, 1], rs_s.at[c], (me, sibling))
+
+    def part(c, slot, half):
+        return term.at[c, slot, core, pl.ds(half * HALF, HALF)]
 
     def send_f(c, i):
         return remote(
-            part(c, 2, i), rv_f.at[c, i], ss_d.at[c], rs_f.at[c, i],
+            part(c, 3, i), rv_f.at[c, i], ss_d.at[c, 0], rs_f.at[c, i],
             (me, head_at(1 if i == 0 else 3)),
         )
 
     def send_n(c, i, half):
         dy = 1 if i == 0 else 3
         return remote(
-            part(c, dy, half), rv_n.at[c, i, pl.ds(half * HALF, HALF)],
-            ss_d.at[c], rs_n.at[c], (me, head_at(dy)),
+            part(c, 1 + i, half), rv_n.at[c, i, pl.ds(half * HALF, HALF)],
+            ss_d.at[c, 0], rs_n.at[c], (me, head_at(dy)),
         )
 
     def out_project(c):
         for side in range(2):
             p = 1 - core if side == 0 else core
 
-            at = pl.ds(pl.multiple_of(c * CC, 128), CC)
-            rows = ah[pl.ds(pl.multiple_of(p * (ALL // 2), BLOCK), ALL // 2), :]
+            at = pl.ds(pl.multiple_of(c * CD, 128), CD)
+            rows = ah[:, p].reshape(ALL // 2, ATT + HID)
             got = jnp.dot(rows, wo[:, at], preferred_element_type=F32).astype(BF16)
-            term[c, p] = got.reshape(Y, ROWS, CC)
+            term[c, :, p] = got.reshape(Y, ROWS, CD)
             if side == 0:
                 send_s(c).start()
 
     def pair_sum(c):
         send_s(c).wait_recv()
 
-        def add(i, carry):
-            term[c, core, i] = (term[c, core, i].astype(F32) + rv_s[c, i].astype(F32)).astype(BF16)
-            return carry
-
-        lax.fori_loop(0, Y, add, 0)
+        def add(i):
+            term[c, i, core] = (term[c, i, core].astype(F32) + rv_s[c, i].astype(F32)).astype(BF16)
+
+        add(3)
         send_f(c, 0).start()
         send_f(c, 1).start()
+        add(1)
         send_n(c, 0, 1).start()
+        add(2)
         send_n(c, 1, 0).start()
+        add(0)
 
     def relay(c):
         for i in range(2):
             send_f(c, i).wait_recv()
-            ref = part(c, 1 if i == 0 else 3, i)
+            ref = part(c, 1 + i, i)
             ref[...] = (ref[...].astype(F32) + rv_f[c, i].astype(F32)).astype(BF16)
             send_n(c, i, i).start()
 
@@ -344,11 +373,11 @@
 
     def finish(c):
         arrived(rv_n.at[c], rs_n.at[c])
-        cols = pl.ds(pl.multiple_of(c * CC, 128), CC)
+        cols = pl.ds(pl.multiple_of(c * CD, 128), CD)
         for r in range(RCAP):
             at = slice(r * BLOCK, (r + 1) * BLOCK)
             total = (
-                term[c, core, y, at, :].astype(F32)
+                term[c, 0, core, at, :].astype(F32)
                 + rv_n[c, 0, at, :].astype(F32)
                 + rv_n[c, 1, at, :].astype(F32)
             )
@@ -364,40 +393,47 @@
         rv_e[c, me] = st_e[c, me]
 
     def second_half(t, carry):
-        @pl.when(t < NC)
+        @pl.when(t < ND)
         def _():
             out_project(t)
 
         for lag, step in zip(LAG_D, (pair_sum, relay, finish), strict=True):
 
-            @pl.when(jnp.logical_and(t >= lag, t < NC + lag))
+            @pl.when(jnp.logical_and(t >= lag, t < ND + lag))
             def _(lag=lag, step=step):
                 step(t - lag)
 
         return carry
 
-    lax.fori_loop(0, NC + LAG_D[-1], second_half, 0)
+    lax.fori_loop(0, ND + LAG_D[-1], second_half, 0)
 
     def collect(c, carry):
         arrived(rv_e.at[c, pl.ds(0, PEERS)], rs_e.at[c])
-        inbox[...] = rv_e[c]
-        cols = pl.ds(pl.multiple_of(c * CC, 128), CC)
+        outbox[...] = rv_e[c]
+        cols = pl.ds(pl.multiple_of(c * CD, 128), CD)
         for j in range(BLK_DEV):
             at = slice(j * BLOCK, (j + 1) * BLOCK)
-            back = inbox[targets[j]].astype(F32)
+            back = outbox[targets[j]].astype(F32)
             out[at, cols] = (tok[at, cols].astype(F32) + back).astype(BF16)
         return carry
 
-    lax.fori_loop(0, NC, collect, 0)
-
-    def drain(c, carry):
+    lax.fori_loop(0, ND, collect, 0)
+
+    def drain_a(c, carry):
         left(st_a.at[c, pl.ds(0, PEERS)], ss_a.at[c])
+        left(gath.at[c, pl.ds(0, 3), 0], ss_b.at[c, 0])
+        left(gath.at[c, :, 0], ss_b.at[c, 1])
+        return carry
+
+    lax.fori_loop(0, NC, drain_a, 0)
+
+    def drain_d(c, carry):
         left(st_e.at[c, pl.ds(0, PEERS)], ss_e.at[c])
-        left(gath.at[c, pl.ds(0, 7)], ss_b.at[c])
-        left(gath.at[c, pl.ds(0, 7)], ss_d.at[c])
-        return carry
-
-    lax.fori_loop(0, NC, drain, 0)
+        left(term.at[c, pl.ds(0, 3), 0], ss_d.at[c, 0])
+        left(term.at[c, :, 0], ss_d.at[c, 1])
+        return carry
+
+    lax.fori_loop(0, ND, drain_d, 0)
 
 
 def body(
@@ -416,31 +452,32 @@
         scratch_shapes=[
             pltpu.VMEM((BLK_DEV, BLOCK, D), BF16),
             pltpu.VMEM((NSEQ, BLOCK, CC), BF16),
+            pltpu.VMEM((NSEQ, BLOCK, CD), BF16),
             pltpu.VMEM((NC, NSEQ, BLOCK, CC), BF16),
             pltpu.VMEM((NC, NSEQ, BLOCK, CC), BF16),
-            pltpu.VMEM((NC, NHEAD, ROWS, CC), BF16),
+            pltpu.VMEM((NC, Y, 2, ROWS, CC), BF16),
             pltpu.VMEM((2, D, HID), BF16),
             pltpu.VMEM((ATT + HID, D), BF16),
             pltpu.VMEM((2, ALL, HID), F32),
             pltpu.VMEM((2, ALL, 2 * HD), BF16),
             pltpu.VMEM((2, ALL, 2 * HD), BF16),
             pltpu.VMEM((2, ALL, 2 * HD), BF16),
-            pltpu.VMEM((ALL, ATT + HID), BF16),
-            pltpu.VMEM((NC, 2, Y, ROWS, CC), BF16),
-            pltpu.VMEM((NC, Y, ROWS, CC), BF16),
-            pltpu.VMEM((NC, 2, HALF, CC), BF16),
-            pltpu.VMEM((NC, 2, ROWS, CC), BF16),
-            pltpu.VMEM((NC, RCAP, BLOCK, CC), BF16),
-            pltpu.VMEM((NC, NSEQ, BLOCK, CC), BF16),
-            pltpu.VMEM((NC, NSEQ, BLOCK, CC), BF16),
+            pltpu.VMEM((Y, 2, ROWS, ATT + HID), BF16),
+            pltpu.VMEM((ND, Y, 2, ROWS, CD), BF16),
+            pltpu.VMEM((ND, Y, ROWS, CD), BF16),
+            pltpu.VMEM((ND, 2, HALF, CD), BF16),
+            pltpu.VMEM((ND, 2, ROWS, CD), BF16),
+            pltpu.VMEM((ND, RCAP, BLOCK, CD), BF16),
+            pltpu.VMEM((ND, NSEQ, BLOCK, CD), BF16),
+            pltpu.VMEM((ND, NSEQ, BLOCK, CD), BF16),
             pltpu.SMEM((NSEQ,), jnp.int32),
             pltpu.SMEM((RCAP,), jnp.int32),
             pltpu.SMEM((RCAP,), jnp.int32),
             dma((6,)),
             dma((NC,)), dma((NC,)),
-            dma((NC,)), dma((NC, Y - 1)), dma((NC,)),
-            dma((NC,)), dma((NC,)), dma((NC, 2)), dma((NC,)),
-            dma((NC,)), dma((NC,)),
+            dma((NC, 2)), dma((NC, Y - 1)), dma((NC, 2)),
+            dma((ND, 2)), dma((ND,)), dma((ND, 2)), dma((ND,)),
+            dma((ND,)), dma((ND,)),
         ],
         compiler_params=pltpu.CompilerParams(
             collective_id=0, has_side_effects=True, vmem_limit_bytes=62 << 20

time: 84.3 us -> 82.1 us (0.974)
  Pallas kernels: 82.4 us -> 80.2 us
    pallas_call x1, Pallas kernels: 82.4 us -> 80.2 us  [body(): pl.pallas_call(kernel, out_shape=jax.ShapeDtypeStruct((BLK_DEV * BLOCK, D...]
where the time goes in v3:
time: 82.1 us; the launch traced here: 81.9 us
  Pallas kernels  80.2 us (98%)
  local copies, waits for them, and re-layouts  1.77 us (2%)
    pallas_call x1, Pallas kernels, body(): pl.pallas_call(kernel, out_shape=jax.ShapeDtypeStruct((BLK_DEV * BLOCK, D...  80.2 us
    unnamed x1, local copies, waits for them, and re-layouts  1.77 us

profile of v3, /device:TPU:0, one launch (start us, length us, event | category | flops | bytes accessed | tf_op | source)
XLA Modules:
  0.0 81.9 jit_solution(14974838418224156186)
XLA Ops:
  0.0 80.2 %shard_map.82 = bf16[64,3072]{1,0:T(8,128)(2,1)} custom-call(s32[512]{0:T(512)} %bt.1, s32[512]{0:T(512)} %cw.1, bf16[64,3072]{1,0:T(8,128)(2,1)} %tok.1, f32[3,4,3072]{2,1,0:T(4,128)} %bitcast.3, bf16[3,3072,256]{2,1,0:T(8,128)(2,1)} %bitcast.2, bf16[3072,768]{1,0:T(8,128)(2,1)} %wh.1, bf16[256,3072]{1,0:T(8,128)(2,1)} %woa.1, bf16[768,3072]{1,0:T(8,128)(2,1)} %woh.1), custom_call_target="tpu_custom_call" | custom-call | flops 12999999488 | bytes 17000000 | tf_op jit(solution)/shard_map/pallas_call | solution.py:447
  80.2 1.8 %copy.10 = bf16[64,3072]{1,0:T(8,128)(2,1)} copy(bf16[64,3072]{1,0:T(8,128)(2,1)} %shard_map.82) | data formatting | bytes 786432

commit v4 on v3

--- a/solution.py
+++ b/solution.py
@@ -27,10 +27,10 @@
 ROWS = RCAP * BLOCK
 ALL = NHEAD * ROWS
 HALF = ROWS // 2
-NC = 6
-CC = D // NC
-ND = 6
-CD = D // ND
+FIRST = (2, 4, 4, 4, 4, 4, 2)
+SECOND = (4, 4, 4, 4, 4, 4)
+NC = len(FIRST)
+ND = len(SECOND)
 QT = ALL // 2
 ATT = 256
 HID = 768
@@ -40,9 +40,17 @@
 AHEAD = 3
 LAG_B = (1, 3, 2)
 LAG_D = (1, 2, 3)
-BIG = 1536.0
+BIG = 256.0
 EXP_A = HD ** (-0.5) * math.log2(math.e)
-EXP_B = BIG * EXP_A
+
+
+def spans(widths):
+    starts = [128 * sum(widths[:i]) for i in range(len(widths))]
+    return [slice(a, a + 128 * w) for a, w in zip(starts, widths, strict=True)]
+
+
+COLS = spans(FIRST)
+BACK = spans(SECOND)
 
 OFFSETS = sorted(
     [(a, b) for a in range(Z) for b in range(X) if (a, b) != (0, 0)],
@@ -110,9 +118,7 @@
         pick = jnp.int32(0)
         for j in range(1, BLK_DEV):
             pick = jnp.where(targets[j] == t, j, pick)
-        block = nrm[pick]
-        for c in range(NC):
-            st_a[c, t] = block[:, c * CC : (c + 1) * CC]
+        st_a[t] = nrm[pick]
         return carry
 
     lax.fori_loop(0, NSEQ, stage, 0)
@@ -120,15 +126,14 @@
 
     def send_a(c, k):
         to = seq_at(*OFFSETS[k])
-        return remote(st_a.at[c, to], rv_a.at[c, me], ss_a.at[c], rs_a.at[c], (to, head))
+        return remote(st_a.at[to, :, COLS[c]], rv_a.at[me, :, COLS[c]], ss_a.at[c], rs_a.at[c], (to, head))
 
     def start_a(c):
         for k in range(PEERS):
             send_a(c, k).start()
-        rv_a[c, me] = st_a[c, me]
-
-    for c in range(AHEAD):
-        start_a(c)
+        rv_a[me, :, COLS[c]] = st_a[me, :, COLS[c]]
+
+    start_a(0)
 
     def entry(s, h):
         live, clip = jnp.int32(0), jnp.int32(0)
@@ -170,11 +175,12 @@
         dead = (jnp.int32(CPG),) * RCAP
         _, named = lax.fori_loop(0, NSEQ, slot, (jnp.int32(0), dead))
         for r in range(RCAP):
-            one = jnp.where(lanes == named[r], 1.0, 0.0)
+            same = jnp.where(lanes == named[r], 1.0, 0.0)
+            always = jnp.where(lanes == CPG + 1, 1.0, 0.0)
             at = pl.ds(pl.multiple_of(g * ROWS + r * BLOCK, BLOCK), BLOCK)
             for i in range(2):
-                qa[i, at, HD:] = (one * BIG).astype(BF16)
-                ka[i, at, HD:] = one.astype(BF16)
+                qa[i, at, HD:] = ((same - always) * BIG).astype(BF16)
+                ka[i, at, HD:] = (same + always).astype(BF16)
                 va[i, at, HD:] = jnp.ones((BLOCK, HD), BF16)
         return carry
 
@@ -184,37 +190,38 @@
 
     lax.fori_loop(0, 2, clear, 0)
 
+    for c in range(1, AHEAD):
+        start_a(c)
+
     def send_b(c, k):
         return remote(
-            gath.at[c, 0, core], gath.at[c, SLOT[Y - k], core],
+            gath.at[0, core, :, COLS[c]], gath.at[SLOT[Y - k], core, :, COLS[c]],
             ss_b.at[c, 0], rs_b.at[c, k // 2], (me, head_at(k)),
         )
 
     def pass_b(c, k):
         half = pl.ds((k // 2) * HALF, HALF)
         return remote(
-            gath.at[c, SLOT[Y - k], core, half], gath.at[c, SLOT[2], core, half],
+            gath.at[SLOT[Y - k], core, half, COLS[c]], gath.at[SLOT[2], core, half, COLS[c]],
             ss_b.at[c, 0], rs_b.at[c, 2], (me, head_at(k)),
         )
 
     def send_g(c, slot):
-        ref = gath.at[c, slot, core]
+        ref = gath.at[slot, core, :, COLS[c]]
         return remote(ref, ref, ss_b.at[c, 1], rs_g.at[c, slot // 3], (me, sibling))
 
     def arrive(c):
-        arrived(rv_a.at[c, pl.ds(0, PEERS)], rs_a.at[c])
-
-        @pl.when(c + AHEAD < NC)
-        def _():
+        cols = COLS[c]
+        wide = slice(0, cols.stop - cols.start)
+        arrived(rv_a.at[0:PEERS, :, cols], rs_a.at[c])
+        if c + AHEAD < NC:
             start_a(c + AHEAD)
-
-        inbox[...] = rv_a[c]
-        cols = pl.ds(pl.multiple_of(c * CC, 128), CC)
+        inbox[:, :, wide] = rv_a[:, :, cols]
         for r in range(RCAP):
             one = pl.ds(clips[r], 1)
-            rows = inbox[srcs[r]].astype(F32)
+            rows = inbox[srcs[r], :, wide].astype(F32)
             shaped = rows * (1.0 + md[1, one, cols]) + md[0, one, cols]
-            gath[c, 0, core, r * BLOCK : (r + 1) * BLOCK, :] = shaped.astype(BF16)
+            gath[0, core, r * BLOCK : (r + 1) * BLOCK, cols] = shaped.astype(BF16)
         for k in (1, 3):
             send_b(c, k).start()
         send_g(c, 0).start()
@@ -222,22 +229,22 @@
     def forward_near(c):
         for k in (1, 3):
             slot = SLOT[Y - k]
-            arrived(gath.at[c, slot, core], rs_b.at[c, k // 2])
+            arrived(gath.at[slot, core, :, COLS[c]], rs_b.at[c, k // 2])
             pass_b(c, k).start()
             send_g(c, slot).start()
 
     def forward_far(c):
-        arrived(gath.at[c, 3, core], rs_b.at[c, 2])
+        arrived(gath.at[3, core, :, COLS[c]], rs_b.at[c, 2])
         send_g(c, 3).start()
 
     def project_rows(c, slots):
         rows = len(slots) * 2 * ROWS
-        at = pl.ds(pl.multiple_of(c * CC, 128), CC)
+        cols = COLS[c]
         to = pl.ds(slots[0] * 2 * ROWS, rows)
 
         def tile(n, carry):
-            left = gath[c, slots[0] : slots[-1] + 1].reshape(rows, CC)
-            acc[n, to, :] += jnp.dot(left, win[n, at, :], preferred_element_type=F32)
+            lhs = gath[slots[0] : slots[-1] + 1, :, :, cols].reshape(rows, cols.stop - cols.start)
+            acc[n, to, :] += jnp.dot(lhs, win[n, cols, :], preferred_element_type=F32)
             return carry
 
         lax.fori_loop(0, 2, tile, 0)
@@ -249,7 +256,7 @@
         at = pl.ds(pl.multiple_of(b * ROWS, BLOCK), ROWS)
         for i in range(2):
             part = [slice(n * ATT + i * HD, n * ATT + (i + 1) * HD) for n in range(3)]
-            qa[i, at, 0:HD] = rms(acc[0, at, part[0]]).astype(BF16)
+            qa[i, at, 0:HD] = (rms(acc[0, at, part[0]]) * EXP_A).astype(BF16)
             ka[i, at, 0:HD] = rms(acc[0, at, part[1]]).astype(BF16)
             va[i, at, 0:HD] = acc[0, at, part[2]].astype(BF16)
         v = acc[1, at, :]
@@ -258,45 +265,30 @@
         return carry
 
     def project(c):
-        near = gath.at[c, pl.ds(0, 3), 1 - core]
-        far = gath.at[c, 3, 1 - core]
-
-        @pl.when(c < NC - 1)
-        def _():
-            arrived(near, rs_g.at[c, 0])
+        near = gath.at[0:3, 1 - core, :, COLS[c]]
+        far = gath.at[3, 1 - core, :, COLS[c]]
+        arrived(near, rs_g.at[c, 0])
+        if c < NC - 1:
             arrived(far, rs_g.at[c, 1])
             project_rows(c, range(Y))
-
-        @pl.when(c == NC - 1)
-        def _():
-            arrived(near, rs_g.at[c, 0])
-            project_rows(c, range(3))
-            lax.fori_loop(0, NEAR, shape_rows, 0)
-            arrived(far, rs_g.at[c, 1])
-            project_rows(c, range(3, Y))
-            lax.fori_loop(NEAR, NHEAD, shape_rows, 0)
+            return
+        project_rows(c, range(3))
+        lax.fori_loop(0, NEAR, shape_rows, 0)
+        arrived(far, rs_g.at[c, 1])
+        project_rows(c, range(3, Y))
+        lax.fori_loop(NEAR, NHEAD, shape_rows, 0)
 
     for i in range(4):
         loads[i].wait()
 
-    def first_half(t, carry):
-        @pl.when(t < NC)
-        def _():
+    for t in range(NC + max(LAG_B)):
+        if t < NC:
             arrive(t)
-
-        @pl.when(t < NHEAD)
-        def _():
+        if t < NHEAD:
             group_slots(t, 0)
-
         for lag, step in zip(LAG_B, (forward_near, project, forward_far), strict=True):
-
-            @pl.when(jnp.logical_and(t >= lag, t < NC + lag))
-            def _(lag=lag, step=step):
+            if lag <= t < NC + lag:
                 step(t - lag)
-
-        return carry
-
-    lax.fori_loop(0, NC + max(LAG_B), first_half, 0)
 
     def attend(b, carry):
         at = pl.ds(pl.multiple_of(b * QT, QT), QT)
@@ -304,7 +296,7 @@
             scores = lax.dot_general(
                 qa[i, at, :], ka[i], (((1,), (1,)), ((), ())), preferred_element_type=F32
             )
-            powers = jnp.exp2(scores * EXP_A - EXP_B).astype(BF16)
+            powers = jnp.exp2(scores).astype(BF16)
             mixed = jnp.dot(powers, va[i], preferred_element_type=F32)
             found = (mixed[:, 0:HD] / mixed[:, HD:]).astype(BF16)
             ah[pl.ds(b * 2, 2), :, :, i * HD : (i + 1) * HD] = found.reshape(2, 2, ROWS, HD)
@@ -316,21 +308,22 @@
         loads[i].wait()
 
     def send_s(c):
-        return remote(term.at[c, :, 1 - core], rv_s.at[c], ss_d.at[c, 1], rs_s.at[c], (me, sibling))
+        ref = term.at[:, 1 - core, :, BACK[c]]
+        return remote(ref, rv_s.at[:, :, BACK[c]], ss_d.at[c, 1], rs_s.at[c], (me, sibling))
 
     def part(c, slot, half):
-        return term.at[c, slot, core, pl.ds(half * HALF, HALF)]
+        return term.at[slot, core, pl.ds(half * HALF, HALF), BACK[c]]
 
     def send_f(c, i):
         return remote(
-            part(c, 3, i), rv_f.at[c, i], ss_d.at[c, 0], rs_f.at[c, i],
+            part(c, 3, i), rv_f.at[i, :, BACK[c]], ss_d.at[c, 0], rs_f.at[c, i],
             (me, head_at(1 if i == 0 else 3)),
         )
 
     def send_n(c, i, half):
         dy = 1 if i == 0 else 3
         return remote(
-            part(c, 1 + i, half), rv_n.at[c, i, pl.ds(half * HALF, HALF)],
+            part(c, 1 + i, half), rv_n.at[i, pl.ds(half * HALF, HALF), BACK[c]],
             ss_d.at[c, 0], rs_n.at[c], (me, head_at(dy)),
         )
 
@@ -338,10 +331,10 @@
         for side in range(2):
             p = 1 - core if side == 0 else core
 
-            at = pl.ds(pl.multiple_of(c * CD, 128), CD)
+            cols = BACK[c]
             rows = ah[:, p].reshape(ALL // 2, ATT + HID)
-            got = jnp.dot(rows, wo[:, at], preferred_element_type=F32).astype(BF16)
-            term[c, :, p] = got.reshape(Y, ROWS, CD)
+            got = jnp.dot(rows, wo[:, cols], preferred_element_type=F32).astype(BF16)
+            term[:, p, :, cols] = got.reshape(Y, ROWS, cols.stop - cols.start)
             if side == 0:
                 send_s(c).start()
 
@@ -349,7 +342,8 @@
         send_s(c).wait_recv()
 
         def add(i):
-            term[c, i, core] = (term[c, i, core].astype(F32) + rv_s[c, i].astype(F32)).astype(BF16)
+            both = term[i, core, :, BACK[c]].astype(F32) + rv_s[i, :, BACK[c]].astype(F32)
+            term[i, core, :, BACK[c]] = both.astype(BF16)
 
         add(3)
         send_f(c, 0).start()
@@ -364,76 +358,58 @@
         for i in range(2):
             send_f(c, i).wait_recv()
             ref = part(c, 1 + i, i)
-            ref[...] = (ref[...].astype(F32) + rv_f[c, i].astype(F32)).astype(BF16)
+            ref[...] = (ref[...].astype(F32) + rv_f[i, :, BACK[c]].astype(F32)).astype(BF16)
             send_n(c, i, i).start()
 
     def send_e(c, k):
         to = seq_at(*OFFSETS[k])
-        return remote(st_e.at[c, to], rv_e.at[c, me], ss_e.at[c], rs_e.at[c], (to, head))
+        return remote(st_e.at[to, :, BACK[c]], rv_e.at[me, :, BACK[c]], ss_e.at[c], rs_e.at[c], (to, head))
 
     def finish(c):
-        arrived(rv_n.at[c], rs_n.at[c])
-        cols = pl.ds(pl.multiple_of(c * CD, 128), CD)
+        cols = BACK[c]
+        arrived(rv_n.at[:, :, cols], rs_n.at[c])
         for r in range(RCAP):
             at = slice(r * BLOCK, (r + 1) * BLOCK)
             total = (
-                term[c, 0, core, at, :].astype(F32)
-                + rv_n[c, 0, at, :].astype(F32)
-                + rv_n[c, 1, at, :].astype(F32)
+                term[0, core, at, cols].astype(F32)
+                + rv_n[0, at, cols].astype(F32)
+                + rv_n[1, at, cols].astype(F32)
             )
-            fin[c, r] = (total * md[2, pl.ds(clips[r], 1), cols]).astype(BF16)
+            fin[r, :, cols] = (total * md[2, pl.ds(clips[r], 1), cols]).astype(BF16)
 
         def stage_back(t, carry):
-            st_e[c, t] = fin[c, ranks[t]]
+            st_e[t, :, cols] = fin[ranks[t], :, cols]
             return carry
 
         lax.fori_loop(0, NSEQ, stage_back, 0)
         for k in range(PEERS):
             send_e(c, k).start()
-        rv_e[c, me] = st_e[c, me]
-
-    def second_half(t, carry):
-        @pl.when(t < ND)
-        def _():
+        rv_e[me, :, cols] = st_e[me, :, cols]
+
+    for t in range(ND + max(LAG_D)):
+        if t < ND:
             out_project(t)
-
         for lag, step in zip(LAG_D, (pair_sum, relay, finish), strict=True):
-
-            @pl.when(jnp.logical_and(t >= lag, t < ND + lag))
-            def _(lag=lag, step=step):
+            if lag <= t < ND + lag:
                 step(t - lag)
 
-        return carry
-
-    lax.fori_loop(0, ND + LAG_D[-1], second_half, 0)
-
-    def collect(c, carry):
-        arrived(rv_e.at[c, pl.ds(0, PEERS)], rs_e.at[c])
-        outbox[...] = rv_e[c]
-        cols = pl.ds(pl.multiple_of(c * CD, 128), CD)
+    for c, cols in enumerate(BACK):
+        arrived(rv_e.at[0:PEERS, :, cols], rs_e.at[c])
+        wide = slice(0, cols.stop - cols.start)
+        outbox[:, :, wide] = rv_e[:, :, cols]
         for j in range(BLK_DEV):
             at = slice(j * BLOCK, (j + 1) * BLOCK)
-            back = outbox[targets[j]].astype(F32)
+            back = outbox[targets[j], :, wide].astype(F32)
             out[at, cols] = (tok[at, cols].astype(F32) + back).astype(BF16)
-        return carry
-
-    lax.fori_loop(0, ND, collect, 0)
-
-    def drain_a(c, carry):
-        left(st_a.at[c, pl.ds(0, PEERS)], ss_a.at[c])
-        left(gath.at[c, pl.ds(0, 3), 0], ss_b.at[c, 0])
-        left(gath.at[c, :, 0], ss_b.at[c, 1])
-        return carry
-
-    lax.fori_loop(0, NC, drain_a, 0)
-
-    def drain_d(c, carry):
-        left(st_e.at[c, pl.ds(0, PEERS)], ss_e.at[c])
-        left(term.at[c, pl.ds(0, 3), 0], ss_d.at[c, 0])
-        left(term.at[c, :, 0], ss_d.at[c, 1])
-        return carry
-
-    lax.fori_loop(0, ND, drain_d, 0)
+
+    for c, cols in enumerate(COLS):
+        left(st_a.at[0:PEERS, :, cols], ss_a.at[c])
+        left(gath.at[0:3, 0, :, cols], ss_b.at[c, 0])
+        left(gath.at[:, 0, :, cols], ss_b.at[c, 1])
+    for c, cols in enumerate(BACK):
+        left(st_e.at[0:PEERS, :, cols], ss_e.at[c])
+        left(term.at[0:3, 0, :, cols], ss_d.at[c, 0])
+        left(term.at[:, 0, :, cols], ss_d.at[c, 1])
 
 
 def body(
@@ -451,11 +427,11 @@
         out_specs=vmem,
         scratch_shapes=[
             pltpu.VMEM((BLK_DEV, BLOCK, D), BF16),
-            pltpu.VMEM((NSEQ, BLOCK, CC), BF16),
-            pltpu.VMEM((NSEQ, BLOCK, CD), BF16),
-            pltpu.VMEM((NC, NSEQ, BLOCK, CC), BF16),
-            pltpu.VMEM((NC, NSEQ, BLOCK, CC), BF16),
-            pltpu.VMEM((NC, Y, 2, ROWS, CC), BF16),
+            pltpu.VMEM((NSEQ, BLOCK, 128 * max(FIRST)), BF16),
+            pltpu.VMEM((NSEQ, BLOCK, 128 * max(SECOND)), BF16),
+            pltpu.VMEM((NSEQ, BLOCK, D), BF16),
+            pltpu.VMEM((NSEQ, BLOCK, D), BF16),
+            pltpu.VMEM((Y, 2, ROWS, D), BF16),
             pltpu.VMEM((2, D, HID), BF16),
             pltpu.VMEM((ATT + HID, D), BF16),
             pltpu.VMEM((2, ALL, HID), F32),
@@ -463,13 +439,13 @@
             pltpu.VMEM((2, ALL, 2 * HD), BF16),
             pltpu.VMEM((2, ALL, 2 * HD), BF16),
             pltpu.VMEM((Y, 2, ROWS, ATT + HID), BF16),
-            pltpu.VMEM((ND, Y, 2, ROWS, CD), BF16),
-            pltpu.VMEM((ND, Y, ROWS, CD), BF16),
-            pltpu.VMEM((ND, 2, HALF, CD), BF16),
-            pltpu.VMEM((ND, 2, ROWS, CD), BF16),
-            pltpu.VMEM((ND, RCAP, BLOCK, CD), BF16),
-            pltpu.VMEM((ND, NSEQ, BLOCK, CD), BF16),
-            pltpu.VMEM((ND, NSEQ, BLOCK, CD), BF16),
+            pltpu.VMEM((Y, 2, ROWS, D), BF16),
+            pltpu.VMEM((Y, ROWS, D), BF16),
+            pltpu.VMEM((2, HALF, D), BF16),
+            pltpu.VMEM((2, ROWS, D), BF16),
+            pltpu.VMEM((RCAP, BLOCK, D), BF16),
+            pltpu.VMEM((NSEQ, BLOCK, D), BF16),
+            pltpu.VMEM((NSEQ, BLOCK, D), BF16),
             pltpu.SMEM((NSEQ,), jnp.int32),
             pltpu.SMEM((RCAP,), jnp.int32),
             pltpu.SMEM((RCAP,), jnp.int32),

time: 82.1 us -> 81.7 us (level)
  no operation moved by 1% of the time
where the time goes in v4:
time: 81.7 us; the launch traced here: 81.5 us
  Pallas kernels  79.8 us (98%)
  local copies, waits for them, and re-layouts  1.77 us (2%)
    pallas_call x1, Pallas kernels, body(): pl.pallas_call(kernel, out_shape=jax.ShapeDtypeStruct((BLK_DEV * BLOCK, D...  79.8 us
    unnamed x1, local copies, waits for them, and re-layouts  1.77 us

profile of v4, /device:TPU:0, one launch (start us, length us, event | category | flops | bytes accessed | tf_op | source)
XLA Modules:
  0.0 81.5 jit_solution(2236365490487532)
XLA Ops:
  0.0 79.8 %shard_map.82 = bf16[64,3072]{1,0:T(8,128)(2,1)} custom-call(s32[512]{0:T(512)} %bt.1, s32[512]{0:T(512)} %cw.1, bf16[64,3072]{1,0:T(8,128)(2,1)} %tok.1, f32[3,4,3072]{2,1,0:T(4,128)} %bitcast.3, bf16[3,3072,256]{2,1,0:T(8,128)(2,1)} %bitcast.2, bf16[3072,768]{1,0:T(8,128)(2,1)} %wh.1, bf16[256,3072]{1,0:T(8,128)(2,1)} %woa.1, bf16[768,3072]{1,0:T(8,128)(2,1)} %woh.1), custom_call_target="tpu_custom_call" | custom-call | flops 12999999488 | bytes 17000000 | tf_op jit(solution)/shard_map/pallas_call | solution.py:423
  79.8 1.8 %copy.10 = bf16[64,3072]{1,0:T(8,128)(2,1)} copy(bf16[64,3072]{1,0:T(8,128)(2,1)} %shard_map.82) | data formatting | bytes 786432
